TPU v7x, 512 devices: a whole 4x4x16 slice. The times are simulated.
512 devices in a mesh: tensor: 8 (over y, core), prefix: 4 (over x), cont: 16 (over z).
Axes of the slice: x: 4, y: 4, z: 16, core: 2. Of those that a mesh axis runs over, the one named last changes fastest.
Arguments:
- states: bfloat16 [64, 128, 8192], P('cont', None, 'prefix'), may hold values from -12 to 12
- norm_gain: float32 [8192], P('prefix'), may hold values from 0.1 to 1.9
- query_weight: bfloat16 [8192, 8192], P(('prefix', 'cont'), 'tensor'), may hold values from -0.0625 to 0.0625
- key_weight: bfloat16 [8192, 1024], P(('prefix', 'cont'), 'tensor'), may hold values from -0.125 to 0.125
- value_weight: bfloat16 [8192, 1024], P(('prefix', 'cont'), 'tensor'), may hold values from -0.0625 to 0.0625
- prefix_keys: bfloat16 [4, 2048, 8, 128], P('prefix', 'cont', 'tensor'), may hold values from -160 to 160
- prefix_values: bfloat16 [4, 2048, 8, 128], P('prefix', 'cont', 'tensor'), may hold values from -6 to 6
- path_prefix: int32 [64], P('cont'), may hold values from 0 to 3
- out_weight: bfloat16 [8192, 8192], P('tensor', ('prefix', 'cont')), may hold values from -0.0625 to 0.0625
- final_gain: float32 [4, 2048], P('prefix', 'tensor'), may hold values from 0.1 to 1.9
- head_weight: bfloat16 [4, 2048, 8192], P('prefix', 'tensor', 'cont'), may hold values from -3 to 3
- targets: int32 [64, 8], P(('tensor', 'prefix')), may hold values from 0 to 8191
- questions: int32 [64, 1], replicated, may hold values from 0 to 7
Outputs:
- context: bfloat16 [16, 4, 128, 8192], P('cont', 'prefix', None, 'tensor')
- scored_hidden: bfloat16 [64, 8, 4, 2048], P('cont', None, 'prefix', 'tensor')
- token_logprob: float32 [64, 8], P(('tensor', 'prefix'))
- path_score: float32 [64], P(('tensor', 'prefix'))
- question_score: float32 [8], replicated
Inputs may be any that keep to these rules, and one draw needn't show every extreme that they name: Every one of the 8 questions has at least one path.
All inputs are finite; a program needn't handle non-finite values.
Results may differ from a plain program's by a relative error of at most 0.018.
The roundings to bfloat16 on the way count: a program that leaves them out, or rounds other values in their place, can miss the bound.
Values may be sent and summed in bfloat16 or wider, within the bound.
No kernel may reach another device: no remote copies, remote signals or barrier semaphores. Data moves between devices by JAX's collectives and lax.ppermute only.
A program may use at most 128 MiB of HBM per device.

v0:
```python
import math

import jax
import jax.numpy as jnp
from jax import lax
from jax.sharding import PartitionSpec as P

SCORED = 8
QUESTIONS = 8


epsilon = 1e-05
rope_base = 500000.0
far_below = -1e30


def joined(array, axis, combine):
    everything = jax.tree.map(lambda part: lax.all_gather(part, axis), array)
    first = jax.tree.map(lambda part: part[0], everything)

    def lap(k, so_far):
        return combine(so_far, jax.tree.map(lambda part: part[k], everything))

    return lax.fori_loop(1, lax.axis_size(axis), lap, first)


def rotate(vectors, positions):
    half_dim = vectors.shape[-1] // 2
    ladder = jnp.arange(half_dim, dtype=jnp.float32) * (2.0 / vectors.shape[-1])
    inverse = jnp.exp(-math.log(rope_base) * ladder)
    angles = positions.astype(jnp.float32)[:, None] * inverse[None, :]
    cosine = jnp.cos(angles)[:, None, :]
    sine_part = jnp.sin(angles)[:, None, :]
    first_half = vectors[..., :half_dim]
    second_half = vectors[..., half_dim:]
    return jnp.concatenate(
        [
            first_half * cosine - second_half * sine_part,
            second_half * cosine + first_half * sine_part,
        ],
        axis=-1,
    )


def absorb(carried, grouped, key_block, value_block, allowed):
    highest, weight_sum, gathered = carried
    score_pattern = "sqkgd,snkd->skgqn"
    value_pattern = "skgqn,snkd->skgqd"
    scores = jnp.einsum(score_pattern, grouped, key_block, preferred_element_type=jnp.float32) * (
        1.0 / math.sqrt(grouped.shape[-1])
    )
    if allowed is not None:
        scores = jnp.where(allowed, scores, far_below)
    new_peak = jnp.maximum(highest, jnp.max(scores, axis=-1))
    raised = jnp.exp(scores - new_peak[..., None])
    fading = jnp.exp(highest - new_peak)
    weight_sum = weight_sum * fading + jnp.sum(raised, axis=-1)
    gathered = gathered * fading[..., None] + jnp.einsum(
        value_pattern, raised.astype(jnp.bfloat16), value_block, preferred_element_type=jnp.float32
    )
    return (new_peak, weight_sum, gathered)


def body(
    states,
    norm_gain,
    query_weight,
    key_weight,
    value_weight,
    prefix_keys,
    prefix_values,
    path_prefix,
    out_weight,
    final_gain,
    head_weight,
    targets,
    questions,
):
    path_count, path_length, width_block = states.shape
    head_width = prefix_keys.shape[-1]
    key_heads = prefix_keys.shape[2]
    query_heads = query_weight.shape[1] // head_width
    group_size = query_heads // key_heads
    prefix_axis = lax.axis_size("prefix")
    my_prefix = lax.axis_index("prefix")
    full_width = width_block * prefix_axis
    own_paths = path_count // prefix_axis
    prefix_span = prefix_keys.shape[1] * lax.axis_size("cont")
    inputs = states.astype(jnp.float32)
    squares = lax.psum(jnp.sum(inputs * inputs, axis=-1), "prefix")
    scaling = lax.rsqrt(squares / full_width + epsilon)
    row_count = path_count * path_length
    normed = (
        (inputs * scaling[..., None] * norm_gain)
        .astype(jnp.bfloat16)
        .reshape(row_count, width_block)
    )
    pieces = (
        lax.all_gather(query_weight, "cont", axis=0, tiled=True),
        lax.all_gather(key_weight, "cont", axis=0, tiled=True),
        lax.all_gather(value_weight, "cont", axis=0, tiled=True),
    )
    query_part, key_part, value_part = tuple(
        (
            jnp.dot(normed, weight_piece, preferred_element_type=jnp.float32)
            for weight_piece in pieces
        )
    )
    query_sum, key_sum, value_sum = (
        lax.psum_scatter(
            query_part.reshape(path_count, path_length, -1),
            "prefix",
            scatter_dimension=0,
            tiled=True,
        ),
        lax.psum_scatter(
            key_part.reshape(path_count, path_length, -1), "prefix", scatter_dimension=0, tiled=True
        ),
        lax.psum_scatter(
            value_part.reshape(path_count, path_length, -1),
            "prefix",
            scatter_dimension=0,
            tiled=True,
        ),
    )
    positions = prefix_span + jnp.arange(path_length, dtype=jnp.int32)
    queries = rotate(
        query_sum.reshape(own_paths, path_length, query_heads, head_width), positions
    ).astype(jnp.bfloat16)
    fresh_keys = rotate(
        key_sum.reshape(own_paths, path_length, key_heads, head_width), positions
    ).astype(jnp.bfloat16)
    fresh_values = value_sum.reshape(own_paths, path_length, key_heads, head_width).astype(
        jnp.bfloat16
    )
    grouped = queries.reshape(own_paths, path_length, key_heads, group_size, head_width)
    causal = jnp.arange(path_length)[None, :] <= jnp.arange(path_length)[:, None]
    cache_keys, cache_values = (
        lax.all_gather(prefix_keys, "prefix", axis=0, tiled=True),
        lax.all_gather(prefix_values, "prefix", axis=0, tiled=True),
    )
    owners = lax.dynamic_slice_in_dim(path_prefix, my_prefix * own_paths, own_paths)
    selector = (owners[:, None] == jnp.arange(prefix_axis, dtype=jnp.int32)[None, :]).astype(
        jnp.bfloat16
    )
    pieces = (
        lax.all_gather(cache_keys, "cont", axis=1, tiled=True),
        lax.all_gather(cache_values, "cont", axis=1, tiled=True),
    )
    chosen_keys = jnp.einsum(
        "sp,pnkd->snkd", selector, pieces[0], preferred_element_type=jnp.float32
    ).astype(jnp.bfloat16)
    chosen_values = jnp.einsum(
        "sp,pnkd->snkd", selector, pieces[1], preferred_element_type=jnp.float32
    ).astype(jnp.bfloat16)
    carried = absorb(
        (
            jnp.full((own_paths, key_heads, group_size, path_length), far_below, jnp.float32),
            jnp.zeros((own_paths, key_heads, group_size, path_length), jnp.float32),
            jnp.zeros((own_paths, key_heads, group_size, path_length, head_width), jnp.float32),
        ),
        grouped,
        chosen_keys,
        chosen_values,
        None,
    )
    highest, weight_sum, gathered = absorb(carried, grouped, fresh_keys, fresh_values, causal)
    blended = gathered / weight_sum[..., None]
    context_local = (
        blended.transpose(0, 3, 1, 2, 4)
        .reshape(own_paths, path_length, query_heads * head_width)
        .astype(jnp.bfloat16)
    )
    scored_context = context_local[:, path_length - SCORED :, :]
    scored_rows = lax.all_gather(scored_context, "prefix", axis=0, tiled=True).reshape(
        path_count * SCORED, query_heads * head_width
    )
    projected = jnp.dot(
        scored_rows,
        lax.all_gather(out_weight, "cont", axis=1, tiled=True),
        preferred_element_type=jnp.float32,
    )
    projected = lax.psum_scatter(projected, "tensor", scatter_dimension=1, tiled=True)
    sub_width = projected.shape[1]
    residual = lax.dynamic_slice_in_dim(
        states[:, path_length - SCORED :, :], lax.axis_index("tensor") * sub_width, sub_width, 2
    )
    hidden = (
        projected + residual.reshape(path_count * SCORED, sub_width).astype(jnp.float32)
    ).astype(jnp.bfloat16)
    widened = hidden.astype(jnp.float32)
    final_sum = lax.psum(jnp.sum(widened * widened, axis=-1), ("tensor", "prefix"))
    final_normed = (
        widened
        * lax.rsqrt(final_sum / full_width + epsilon)[:, None]
        * final_gain.reshape(sub_width)
    ).astype(jnp.bfloat16)
    every_row = lax.all_gather(final_normed, "cont", axis=0, tiled=True)
    head_block = head_weight.reshape(sub_width, head_weight.shape[2])
    block_rows = targets.shape[0] * targets.shape[1]
    logits = lax.psum_scatter(
        jnp.dot(every_row, head_block, preferred_element_type=jnp.float32),
        ("tensor", "prefix"),
        scatter_dimension=0,
        tiled=True,
    )
    vocab_block = head_block.shape[1]
    offset = lax.axis_index("cont") * vocab_block
    wanted = targets.reshape(block_rows) - offset
    matches = wanted[:, None] == jnp.arange(vocab_block, dtype=jnp.int32)[None, :]
    chosen = jnp.sum(jnp.where(matches, logits, 0.0), axis=-1)
    highest_logit = jnp.max(logits, axis=-1)
    mass_part = jnp.sum(jnp.exp(logits - highest_logit[:, None]), axis=-1)

    def combine(earlier, later):
        summit = jnp.maximum(earlier[0], later[0])
        return (
            summit,
            earlier[1] * jnp.exp(earlier[0] - summit) + later[1] * jnp.exp(later[0] - summit),
            earlier[2] + later[2],
        )

    summit, mass_all, chosen = joined((highest_logit, mass_part, chosen), "cont", combine)
    token_logprob = (chosen - (summit + jnp.log(mass_all))).reshape(targets.shape)
    path_score = jnp.mean(token_logprob, axis=-1)
    local_paths = targets.shape[0]
    block_index = lax.axis_index("tensor") * lax.axis_size("prefix") + lax.axis_index("prefix")
    my_questions = lax.dynamic_slice_in_dim(questions[:, 0], block_index * local_paths, local_paths)
    labels = jnp.arange(QUESTIONS, dtype=jnp.int32)
    member_local = (my_questions[:, None] == labels[None, :]).astype(jnp.float32)
    question_total = lax.psum(
        jnp.sum(member_local * path_score[:, None], axis=0), ("tensor", "prefix")
    )
    member_all = (questions[:, 0][:, None] == labels[None, :]).astype(jnp.float32)
    question_score = question_total / jnp.sum(member_all, axis=0)
    return (
        context_local[None],
        hidden.reshape(path_count, SCORED, 1, sub_width),
        token_logprob,
        path_score,
        question_score,
    )


def solution(mesh):
    in_specs = (
        P("cont", None, "prefix"),
        P("prefix"),
        P(("prefix", "cont"), "tensor"),
        P(("prefix", "cont"), "tensor"),
        P(("prefix", "cont"), "tensor"),
        P("prefix", "cont", "tensor", None),
        P("prefix", "cont", "tensor", None),
        P("cont"),
        P("tensor", ("prefix", "cont")),
        P("prefix", "tensor"),
        P("prefix", "tensor", "cont"),
        P(("tensor", "prefix"), None),
        P(),
    )
    out_specs = (
        P("cont", "prefix", None, "tensor"),
        P("cont", None, "prefix", "tensor"),
        P(("tensor", "prefix"), None),
        P(("tensor", "prefix")),
        P(),
    )
    return jax.shard_map(body, mesh=mesh, in_specs=in_specs, out_specs=out_specs, check_vma=False)
```

profile of v0, /device:TPU:1, one launch (start us, length us, event | category | flops | bytes accessed | tf_op | source)
XLA Modules:
  0.0 669.5 jit_solution(816038582310604199)
XLA Ops:
  8.8 2.1 fusion.10
  10.9 9.3 %psum.21 = f32[4,128]{1,0:T(4,128)S(1)} all-reduce(f32[4,128]{1,0:T(4,128)S(1)} %fusion.10), channel_id=1, replica_groups=mesh['tensor'=8,'prefix'=4,'cont'=16] {'prefix'}, use_global_device_ids=true, to_apply=%region_1.0 | all-reduce | flops 512 | bytes 4096 | tf_op jit(solution)/shard_map/psum | solution.py:90
  20.2 34.8 %all_gather.53 = bf16[2048,128]{1,0:T(8,128)(2,1)S(1)} all-gather(bf16[128,128]{1,0:T(8,128)(2,1)} %param.18), channel_id=1, replica_groups=mesh['tensor'=8,'prefix'=4,'cont'=16] {'cont'}, dimensions={0}, use_global_device_ids=true | all-gather | bytes 557056 | tf_op jit(solution)/shard_map/all_gather | solution.py:100
  55.0 3.1 fusion.34
  58.2 10.4 %all_gather.51 = bf16[4,128,1,128]{3,1,2,0:T(8,128)(2,1)} all-gather(bf16[1,128,1,128]{3,1,2,0:T(8,128)(2,1)S(1)} %copy-done.4), channel_id=1, replica_groups=mesh['tensor'=8,'prefix'=4,'cont'=16] {'prefix'}, dimensions={0}, use_global_device_ids=true | all-gather | bytes 163840 | tf_op jit(solution)/shard_map/all_gather | solution.py:140
  68.7 10.4 %all_gather.48 = bf16[4,128,1,128]{3,1,2,0:T(8,128)(2,1)} all-gather(bf16[1,128,1,128]{3,1,2,0:T(8,128)(2,1)S(1)} %copy-done.5), channel_id=1, replica_groups=mesh['tensor'=8,'prefix'=4,'cont'=16] {'prefix'}, dimensions={0}, use_global_device_ids=true | all-gather | bytes 163840 | tf_op jit(solution)/shard_map/all_gather | solution.py:139
  79.2 11.4 %all-gather.10.cloned.1.call-done = bf16[2048,1024]{1,0:T(8,128)(2,1)} async-done(((bf16[128,1024]{1,0:T(8,128)(2,1)}), bf16[2048,1024]{1,0:T(8,128)(2,1)}) %all-gather.10.cloned.1.call-update) | async-done | bytes 4194320 | tf_op jit(solution)/shard_map/all_gather | solution.py:99
  90.6 5.9 fusion.14
  96.6 24.0 %all_gather.54 = bf16[2048,128]{1,0:T(8,128)(2,1)S(1)} all-gather(bf16[128,128]{1,0:T(8,128)(2,1)S(1)} %copy-done.6), channel_id=1, replica_groups=mesh['tensor'=8,'prefix'=4,'cont'=16] {'cont'}, dimensions={0}, use_global_device_ids=true | all-gather | bytes 557056 | tf_op jit(solution)/shard_map/all_gather | solution.py:101
  125.1 36.1 %all-gather.12.cloned.1.call-done = bf16[4,2048,1,128]{3,1,2,0:T(8,128)(2,1)} async-done(((bf16[4,128,1,128]{3,1,2,0:T(8,128)(2,1)}), bf16[4,2048,1,128]{3,1,2,0:T(8,128)(2,1)}) %all-gather.12.cloned.1.call-update) | async-done | bytes 2097168 | tf_op jit(solution)/shard_map/all_gather | solution.py:148
  161.2 4.9 fusion.18
  166.1 2.3 copy.52
  168.4 64.1 %all-gather.8.cloned.1.call-done = bf16[4,2048,1,128]{3,1,2,0:T(8,128)(2,1)} async-done(((bf16[4,128,1,128]{3,1,2,0:T(8,128)(2,1)}), bf16[4,2048,1,128]{3,1,2,0:T(8,128)(2,1)}) %all-gather.8.cloned.1.call-update) | async-done | bytes 2097168 | tf_op jit(solution)/shard_map/all_gather | solution.py:147
  232.6 5.0 fusion.20
  242.4 2.4 fusion.27
  246.6 9.6 %all_gather.55 = bf16[4,8,1024]{2,1,0:T(8,128)(2,1)S(1)} all-gather(bf16[1,8,1024]{2,1,0:T(8,128)(2,1)S(1)} %copy.59), channel_id=1, replica_groups=mesh['tensor'=8,'prefix'=4,'cont'=16] {'prefix'}, dimensions={0}, use_global_device_ids=true | all-gather | bytes 81920 | tf_op jit(solution)/shard_map/all_gather | solution.py:175
  256.2 69.8 %all-gather.14.cloned.1.call-done = bf16[1024,2048]{1,0:T(8,128)(2,1)} async-done(((bf16[1024,128]{1,0:T(8,128)(2,1)}), bf16[1024,2048]{1,0:T(8,128)(2,1)}) %all-gather.14.cloned.1.call-update) | async-done | bytes 4194320 | tf_op jit(solution)/shard_map/all_gather | solution.py:180
  326.0 3.7 fusion.61
  329.8 42.2 %reduce-scatter.12.cloned.1.call-done = f32[32,256]{1,0:T(8,128)} async-done(((f32[32,2048]{1,0:T(8,128)}), f32[32,256]{1,0:T(8,128)}) %reduce-scatter.12.cloned.1.call-update) | async-done | bytes 32784 | tf_op jit(solution)/shard_map/reduce_scatter | solution.py:183
  372.9 62.8 %psum.22 = f32[32]{0:T(128)S(1)} all-reduce(f32[32]{0:T(128)S(1)} %get-tuple-element.227), channel_id=1, replica_groups=mesh['tensor'=8,'prefix'=4,'cont'=16] {'tensor','prefix'}, use_global_device_ids=true, to_apply=%region_11.12 | all-reduce | flops 32 | bytes 256 | tf_op jit(solution)/shard_map/psum | solution.py:192
  435.7 24.6 %all_gather.57 = bf16[512,256]{1,0:T(8,128)(2,1)S(1)} all-gather(bf16[32,256]{1,0:T(8,128)(2,1)S(1)} %fusion.65), channel_id=1, replica_groups=mesh['tensor'=8,'prefix'=4,'cont'=16] {'cont'}, dimensions={0}, use_global_device_ids=true | all-gather | bytes 278528 | tf_op jit(solution)/shard_map/all_gather | solution.py:198
  463.9 100.4 %reduce-scatter.14.cloned.1.call-done = f32[16,512]{1,0:T(8,128)} async-done(((f32[512,512]{1,0:T(8,128)}), f32[16,512]{1,0:T(8,128)}) %reduce-scatter.14.cloned.1.call-update) | async-done | bytes 32784 | tf_op jit(solution)/shard_map/reduce_scatter | solution.py:201
  566.9 24.1 %all-reduce.3 = (f32[256]{0:T(256)S(1)}, f32[256]{0:T(256)S(1)}, f32[256]{0:T(256)S(1)}) all-reduce(f32[256]{0:T(256)S(1)} %dynamic-update-slice, f32[256]{0:T(256)S(1)} %dynamic-update-slice.1, f32[256]{0:T(256)S(1)} %dynamic-update-slice.2), channel_id=2, replica_groups=mesh['tensor'=8,'prefix'=4,'cont'=16] {'cont'}, use_global_device_ids=true, to_apply=%add | all-reduce | flops 768 | bytes 6144
  593.1 68.5 %psum.23 = f32[8]{0:T(128)S(1)} all-reduce(f32[8]{0:T(128)S(1)} %fusion.73), channel_id=1, replica_groups=mesh['tensor'=8,'prefix'=4,'cont'=16] {'tensor','prefix'}, use_global_device_ids=true, to_apply=%region_20.21 | all-reduce | flops 8 | bytes 64 | tf_op jit(solution)/shard_map/psum | solution.py:231
  (117 shorter events, 21.4 us)
Async XLA Ops:
  8.0 452.4 %copy-start = (bf16[1,256,512]{2,1,0:T(8,128)(2,1)S(1)}, bf16[1,256,512]{2,1,0:T(8,128)(2,1)}, u32[]{:S(2)}) copy-start(bf16[1,256,512]{2,1,0:T(8,128)(2,1)} %param.25) | copy-start | bytes 786436
  8.0 50.1 %copy-start.4 = (bf16[1,128,1,128]{3,1,2,0:T(8,128)(2,1)S(1)}, bf16[1,128,1,128]{3,1,2,0:T(8,128)(2,1)}, u32[]{:S(2)}) copy-start(bf16[1,128,1,128]{3,1,2,0:T(8,128)(2,1)} %param.21) | copy-start | bytes 98308
  8.0 60.7 %copy-start.5 = (bf16[1,128,1,128]{3,1,2,0:T(8,128)(2,1)S(1)}, bf16[1,128,1,128]{3,1,2,0:T(8,128)(2,1)}, u32[]{:S(2)}) copy-start(bf16[1,128,1,128]{3,1,2,0:T(8,128)(2,1)} %param.20) | copy-start | bytes 98308
  8.0 82.6 %copy-start.1 = (bf16[4,128,2048]{2,1,0:T(8,128)(2,1)S(1)}, bf16[4,128,2048]{2,1,0:T(8,128)(2,1)}, u32[]{:S(2)}) copy-start(bf16[4,128,2048]{2,1,0:T(8,128)(2,1)} %param.15) | copy-start | bytes 6291460
  8.0 82.6 %copy-start.10 = (f32[2048]{0:T(1024)S(1)}, f32[2048]{0:T(1024)}, u32[]{:S(2)}) copy-start(f32[2048]{0:T(1024)} %param.16) | copy-start | bytes 24580
  8.1 82.5 %all-gather.10.cloned.1.call-start = ((), (), s32[]{:S(2)}) async-start(), calls=%async_computation.6 | async-start | bytes 4456448 | tf_op jit(solution)/shard_map/all_gather | solution.py:99
  8.8 115.1 %reduce-scatter.8.cloned.1.call-start = ((), (), s32[]{:S(2)}) async-start(), calls=%async_computation.9 | async-start | bytes 327680 | tf_op jit(solution)/shard_map/reduce_scatter | solution.py:116
  58.1 103.1 %all-gather.12.cloned.1.call-start = ((), (), s32[]{:S(2)}) async-start(), calls=%async_computation.8 | async-start | bytes 2228224 | tf_op jit(solution)/shard_map/all_gather | solution.py:148
  68.6 163.9 %all-gather.8.cloned.1.call-start = ((), (), s32[]{:S(2)}) async-start(), calls=%async_computation.5 | async-start | bytes 2228224 | tf_op jit(solution)/shard_map/all_gather | solution.py:147
  79.2 17.4 %copy-start.6 = (bf16[128,128]{1,0:T(8,128)(2,1)S(1)}, bf16[128,128]{1,0:T(8,128)(2,1)}, u32[]{:S(2)}) copy-start(bf16[128,128]{1,0:T(8,128)(2,1)} %param.19) | copy-start | bytes 98308
  79.2 158.4 %reduce-scatter.6.cloned.1.call-start = ((), (), s32[]{:S(2)}) async-start(), calls=%async_computation.7 | async-start | bytes 2621440 | tf_op jit(solution)/shard_map/reduce_scatter | solution.py:110
  96.5 26.4 %copy-start.11 = (s32[4]{0:T(128)S(1)}, s32[4]{0:T(128)}, u32[]{:S(2)}) copy-start(s32[4]{0:T(128)} %param.22) | copy-start | bytes 52
  96.5 148.4 %reduce-scatter.10.cloned.1.call-start = ((), (), s32[]{:S(2)}) async-start(), calls=%async_computation.10 | async-start | bytes 327680 | tf_op jit(solution)/shard_map/reduce_scatter | solution.py:119
  122.1 203.9 %all-gather.14.cloned.1.call-start = ((), (), s32[]{:S(2)}) async-start(), calls=%async_computation.11 | async-start | bytes 4456448 | tf_op jit(solution)/shard_map/all_gather | solution.py:180
  122.6 249.4 %reduce-scatter.12.cloned.1.call-start = ((), (), s32[]{:S(2)}) async-start(), calls=%async_computation.12 | async-start | bytes 294912 | tf_op jit(solution)/shard_map/reduce_scatter | solution.py:183
  237.6 2.0 copy-start.2
  244.9 127.1 %slice-start = ((bf16[4,128,2048]{2,1,0:T(8,128)(2,1)}), bf16[4,8,2048]{2,1,0:T(8,128)(2,1)S(1)}, s32[]{:S(2)}) async-start(bf16[4,128,2048]{2,1,0:T(8,128)(2,1)} %param.15), calls=%async_computation.14 | async-start | bytes 262144 | tf_op jit(solution)/shard_map/slice | solution.py:186
  244.9 190.8 %copy-start.7 = (f32[1,256]{1,0:T(1,128)S(1)}, f32[1,256]{1,0:T(1,128)}, u32[]{:S(2)}) copy-start(f32[1,256]{1,0:T(1,128)} %param.24) | copy-start | bytes 3076
  246.4 215.3 %copy-start.8 = (s32[2,8]{1,0:T(2,128)S(1)}, s32[2,8]{1,0:T(2,128)}, u32[]{:S(2)}) copy-start(s32[2,8]{1,0:T(2,128)} %param.26) | copy-start | bytes 196
  246.4 217.3 %copy-start.12 = (s32[64,1]{0,1:T(1,128)S(1)}, s32[64,1]{0,1:T(1,128)}, u32[]{:S(2)}) copy-start(s32[64,1]{0,1:T(1,128)} %param.27) | copy-start | bytes 772
  329.7 234.6 %reduce-scatter.14.cloned.1.call-start = ((), (), s32[]{:S(2)}) async-start(), calls=%async_computation.13 | async-start | bytes 1081344 | tf_op jit(solution)/shard_map/reduce_scatter | solution.py:201
  372.9 289.3 %copy-start.3 = (bf16[32,256]{1,0:T(8,128)(2,1)}, bf16[32,256]{1,0:T(8,128)(2,1)S(1)}, u32[]{:S(2)}) copy-start(bf16[32,256]{1,0:T(8,128)(2,1)S(1)} %get-tuple-element.228) | copy-start | bytes 49156
  592.1 70.1 %copy-start.9 = (f32[2,8]{1,0:T(2,128)}, f32[2,8]{1,0:T(2,128)S(1)}, u32[]{:S(2)}) copy-start(f32[2,8]{1,0:T(2,128)S(1)} %reshape.383) | copy-start | bytes 196
  592.2 70.0 %copy-start.13 = (f32[2]{0:T(128)}, f32[2]{0:T(128)S(1)}, u32[]{:S(2)}) copy-start(f32[2]{0:T(128)S(1)} %broadcast_multiply_fusion) | copy-start | bytes 28
Sparse Core Ops, SparseCore 0:
  11.2 79.3 all-gather.9
  92.7 68.4 all-gather.11
  163.3 69.2 all-gather.7
  234.6 91.3 all-gather.13
Sparse Core Ops, SparseCore 1:
  58.2 29.6 reduce-scatter.7
  96.6 39.8 reduce-scatter.5
  139.1 26.5 reduce-scatter.9
  329.8 42.1 reduce-scatter.11
  461.8 102.5 reduce-scatter.13
where the time goes:
time: 673 us; the launch traced here: 670 us
  waiting for transfers between devices  325 us (48%)
  blocking collectives  279 us (41%)
  matrix products  30.9 us (5%)
  between operations  16.5 us (2%)
  other arithmetic  9.4 us (1%)
  local copies, waits for them, and re-layouts  7.96 us (1%)
    reduce_scatter x1, waiting for transfers between devices, body(): lax.psum_scatter(jnp.dot(every_row, head_block, preferred_element_type=jn...  100 us
    all_gather x1, waiting for transfers between devices, body(): lax.all_gather(out_weight, 'cont', axis=1, tiled=True)  69.8 us
    psum x1, blocking collectives, body(): lax.psum(jnp.sum(member_local * path_score[:, None], axis=0), ('tensor',...  68.5 us
    all_gather x1, waiting for transfers between devices, body(): lax.all_gather(cache_keys, 'cont', axis=1, tiled=True)  64.1 us
    psum x1, blocking collectives, body(): lax.psum(jnp.sum(widened * widened, axis=-1), ('tensor', 'prefix'))  62.8 us
    reduce_scatter x1, waiting for transfers between devices, body(): lax.psum_scatter(projected, 'tensor', scatter_dimension=1, tiled=True)  42.2 us
    all_gather x1, waiting for transfers between devices, body(): lax.all_gather(cache_values, 'cont', axis=1, tiled=True)  36.1 us
    all_gather x1, blocking collectives, body(): lax.all_gather(key_weight, 'cont', axis=0, tiled=True)  34.8 us
  transfers between devices with their start and end apart: 9, of which 6 were waited for; matrix products, arithmetic and copies ran while one was open for 6% of the time, Pallas kernels for 0%

commit v1 on v0

v1 whole, which is shorter than its diff:
```python
import math

import jax
import jax.numpy as jnp
from jax import lax
from jax.experimental import pallas as pl
from jax.experimental.pallas import tpu as pltpu
from jax.sharding import PartitionSpec as P

SCORED = 8
QUESTIONS = 8
RESIDUES = 2

epsilon = 1e-05
rope_base = 500000.0
far_below = -1e30


def rope_tables(head_width, positions):
    half_dim = head_width // 2
    ladder = jnp.arange(half_dim, dtype=jnp.float32) * (2.0 / head_width)
    inverse = jnp.exp(-math.log(rope_base) * ladder)
    angles = positions.astype(jnp.float32)[:, None] * inverse[None, :]
    cosine, sine = jnp.cos(angles), jnp.sin(angles)
    return jnp.concatenate([cosine, cosine], -1), jnp.concatenate([-sine, sine], -1)


def rotate(vectors, cosine, sine):
    half = vectors.shape[-1] // 2
    swapped = jnp.concatenate([vectors[..., half:], vectors[..., :half]], -1)
    return vectors * cosine + swapped * sine


def attend_kernel(q_ref, cos_ref, sin_ref, kf_ref, vf_ref, kp_ref, vp_ref, out_ref):
    length, width = cos_ref.shape
    heads = q_ref.shape[1] // width
    cosine, sine = cos_ref[...], sin_ref[...]
    turned = []
    for h in range(heads):
        q = q_ref[:, h * width : (h + 1) * width]
        turned.append((q * cosine + pltpu.roll(q, width // 2, 1) * sine).astype(jnp.bfloat16))
    queries = jnp.concatenate(turned, 0)
    contract = (((1,), (1,)), ((), ()))
    old = lax.dot_general(queries, kp_ref[...], contract, preferred_element_type=jnp.float32)
    new = lax.dot_general(queries, kf_ref[...], contract, preferred_element_type=jnp.float32)
    row = lax.broadcasted_iota(jnp.int32, (length, length), 0)
    column = lax.broadcasted_iota(jnp.int32, (length, length), 1)
    allowed = jnp.concatenate([column <= row] * heads, 0)
    new = jnp.where(allowed, new, far_below)
    peak = jnp.maximum(jnp.max(old, -1, keepdims=True), jnp.max(new, -1, keepdims=True))
    factor = math.log2(math.e) / math.sqrt(width)
    old = jnp.exp2((old - peak) * factor)
    new = jnp.exp2((new - peak) * factor)
    total = jnp.sum(old, -1, keepdims=True) + jnp.sum(new, -1, keepdims=True)
    mixed = jnp.dot(old.astype(jnp.bfloat16), vp_ref[...], preferred_element_type=jnp.float32)
    mixed += jnp.dot(new.astype(jnp.bfloat16), vf_ref[...], preferred_element_type=jnp.float32)
    mixed = (mixed / total).astype(jnp.bfloat16)
    for h in range(heads):
        out_ref[:, h * width : (h + 1) * width] = mixed[h * length : (h + 1) * length]


def attend(q, cosine, sine, fresh_keys, fresh_values, keys, values):
    length, columns = q.shape
    width = cosine.shape[1]
    pair = 2 * width
    whole = lambda array: pl.BlockSpec(array.shape, lambda i: (0, 0))
    count = (columns // width) * length * (keys.shape[0] + length)
    return pl.pallas_call(
        attend_kernel,
        grid=(columns // pair,),
        in_specs=[
            pl.BlockSpec((length, pair), lambda i: (0, i)),
            whole(cosine),
            whole(sine),
            whole(fresh_keys),
            whole(fresh_values),
            whole(keys),
            whole(values),
        ],
        out_specs=pl.BlockSpec((length, pair), lambda i: (0, i)),
        out_shape=jax.ShapeDtypeStruct((length, columns), jnp.bfloat16),
        compiler_params=pltpu.CompilerParams(vmem_limit_bytes=40 * 1024 * 1024),
        cost_estimate=pl.CostEstimate(
            flops=4 * count * width, bytes_accessed=2 * 1024 * 1024, transcendentals=count
        ),
    )(q, cosine, sine, fresh_keys, fresh_values, keys, values)


def output_kernel(rows_ref, weight_ref, out_ref):
    pieces, cont_rows, _ = out_ref.shape
    blocks, _, width = weight_ref.shape
    spans = blocks // 2
    rows = rows_ref[...]
    for j in range(blocks):
        product = jnp.dot(rows, weight_ref[j], preferred_element_type=jnp.float32)
        for k in range(pieces // spans):
            out_ref[k * spans + j // 2, :, (j % 2) * width : (j % 2 + 1) * width] = product[
                k * cont_rows : (k + 1) * cont_rows
            ]


def after(array, earlier):
    return lax.optimization_barrier((array, earlier))[0]


def everyone(array, axis, groups=None):
    size = len(groups[0]) if groups else lax.axis_size(axis)
    spread = jnp.broadcast_to(array[None], (size,) + array.shape)
    return lax.all_to_all(spread, axis, 0, 0, axis_index_groups=groups)


def all_conts(array):
    size = lax.axis_size("cont")
    side = math.isqrt(size)
    strided = [[k + side * j for j in range(side)] for k in range(side)]
    beside = [[side * j + k for k in range(side)] for j in range(side)]
    found = everyone(everyone(array, "cont", strided), "cont", beside)
    return jnp.swapaxes(found, 0, 1).reshape((size,) + array.shape)


def body(
    states,
    norm_gain,
    query_weight,
    key_weight,
    value_weight,
    prefix_keys,
    prefix_values,
    path_prefix,
    out_weight,
    final_gain,
    head_weight,
    targets,
    questions,
):
    path_count, path_length, width_block = states.shape
    head_width = prefix_keys.shape[-1]
    tensors, prefixes, conts = (lax.axis_size(a) for a in ("tensor", "prefix", "cont"))
    t, p, c = (lax.axis_index(a) for a in ("tensor", "prefix", "cont"))
    full_width = width_block * prefixes
    prefix_span = prefix_keys.shape[1] * conts
    positions = prefix_span + jnp.arange(path_length, dtype=jnp.int32)
    cosine, sine = rope_tables(head_width, positions)

    lead = jnp.concatenate([key_weight, value_weight, query_weight], 1)
    weights = lax.all_gather(lead, "cont", axis=0, tiled=True)
    gather_cache = lambda cache: lax.all_gather(
        cache.reshape(-1, head_width), "cont", axis=0, tiled=True
    )
    cached_keys, cached_values = gather_cache(prefix_keys), gather_cache(prefix_values)
    near_conts = conts // RESIDUES
    blocks_of = lambda size: [list(range(k, k + size)) for k in range(0, conts, size)]
    window = lax.all_gather(
        after(out_weight, weights),
        "cont",
        axis_index_groups=blocks_of(near_conts),
    )

    inputs = states.astype(jnp.float32)
    squares = jnp.sum(everyone(jnp.sum(inputs * inputs, axis=-1), "prefix"), axis=0)
    scaling = lax.rsqrt(squares / full_width + epsilon)
    normed = (inputs * scaling[..., None] * norm_gain).astype(jnp.bfloat16)
    normed = normed.reshape(path_count * path_length, width_block)

    def project(weight):
        full = jnp.dot(normed, weight, preferred_element_type=jnp.float32)
        return full.reshape(path_count, path_length, -1)

    owner_of = lambda q: lax.dynamic_index_in_dim(path_prefix, q, 0, keepdims=False)
    owner = owner_of(p)
    near = [(i, i ^ 1) for i in range(prefixes)]
    far = [(i, prefixes - 1 - i) for i in range(prefixes)]
    near_p, far_p = p ^ 1, prefixes - 1 - p

    middle = weights.shape[1] // 2
    left_part, right_part = project(weights[:, :middle]), project(weights[:, middle:])

    def choose(mine, first_perm, first_p, second_perm, second_p):
        beside = lax.ppermute(mine, "prefix", first_perm)
        sent = jnp.where(owner_of(second_p) == first_p, beside, mine)
        across = lax.ppermute(sent, "prefix", second_perm)
        across = after(across, left_part)
        return jnp.where(owner == p, mine, jnp.where(owner == first_p, beside, across))

    keys = choose(cached_keys, near, near_p, far, far_p)
    values = choose(cached_values, far, far_p, near, near_p)

    def path_sum(partial, first_perm, first_p, second_perm, second_p):
        pick = lambda q: lax.dynamic_index_in_dim(partial, q, 0, keepdims=False)
        third_p = p ^ first_p ^ second_p
        got = lax.ppermute(jnp.stack([pick(first_p), pick(third_p)]), "prefix", first_perm)
        passed = lax.ppermute(pick(second_p) + got[1], "prefix", second_perm)
        return pick(p) + got[0] + passed

    left = path_sum(left_part, near, near_p, far, far_p)
    right = path_sum(right_part, far, far_p, near, near_p)
    fresh_keys = rotate(left[:, :head_width], cosine, sine).astype(jnp.bfloat16)
    fresh_values = left[:, head_width : 2 * head_width].astype(jnp.bfloat16)
    queries = jnp.concatenate([left[:, 2 * head_width :], right], 1)
    context = attend(queries, cosine, sine, fresh_keys, fresh_values, keys, values)

    scored = context[path_length - SCORED :]
    share = [
        [q * conts + b + k * near_conts for q in range(prefixes) for k in range(RESIDUES)]
        for b in range(near_conts)
    ]
    rows = everyone(scored, ("prefix", "cont"), share)
    rows = rows.reshape(prefixes, RESIDUES, SCORED, -1).transpose(1, 0, 2, 3)
    scored_rows = rows.reshape(RESIDUES * path_count * SCORED, -1)
    cont_rows = path_count * SCORED
    sub_width = 2 * out_weight.shape[1]
    spans = tensors // RESIDUES
    pieces = pl.pallas_call(
        output_kernel,
        out_shape=jax.ShapeDtypeStruct((tensors, cont_rows, sub_width), jnp.float32),
        compiler_params=pltpu.CompilerParams(vmem_limit_bytes=24 * 1024 * 1024),
        cost_estimate=pl.CostEstimate(
            flops=2 * scored_rows.size * window.shape[0] * window.shape[2],
            bytes_accessed=2 * window.size,
            transcendentals=0,
        ),
    )(scored_rows, window)
    summed = jnp.sum(lax.all_to_all(pieces, "tensor", 0, 0), axis=0)
    perm = []
    for k in range(RESIDUES):
        for i in range(spans):
            for a in range(RESIDUES):
                for b in range(near_conts):
                    here = (k * spans + i) * conts + a * near_conts + b
                    perm.append((here, (a * spans + i) * conts + k * near_conts + b))
    summed = lax.ppermute(summed, ("tensor", "cont"), perm)

    residual = lax.dynamic_slice_in_dim(states[:, path_length - SCORED :, :], t * sub_width, sub_width, 2)
    hidden = (summed + residual.reshape(cont_rows, sub_width).astype(jnp.float32)).astype(jnp.bfloat16)

    every = all_conts(hidden).reshape(-1, sub_width).astype(jnp.float32)
    final_part = jnp.sum(every * every, axis=-1, keepdims=True)
    gained = (every * final_gain.reshape(sub_width)).astype(jnp.bfloat16)
    vocab_block = head_weight.shape[2]
    partial = jnp.dot(gained, head_weight.reshape(sub_width, vocab_block), preferred_element_type=jnp.float32)
    high = final_part.astype(jnp.bfloat16)
    low = (final_part - high.astype(jnp.float32)).astype(jnp.bfloat16)
    lanes = 128
    place = jnp.arange(lanes)[None, :]
    extra = jnp.where(place == 0, high, jnp.where(place == 1, low, jnp.zeros_like(high)))
    payload = jnp.concatenate([partial.astype(jnp.bfloat16), extra], 1)
    blocks = tensors * prefixes
    block_rows = targets.shape[0] * targets.shape[1]
    received = lax.all_to_all(
        payload.reshape(blocks, block_rows, vocab_block + lanes), ("tensor", "prefix"), 0, 0
    )
    received = jnp.sum(received.astype(jnp.float32), axis=0)
    final_sum = received[:, vocab_block] + received[:, vocab_block + 1]
    logits = received[:, :vocab_block] * lax.rsqrt(final_sum / full_width + epsilon)[:, None]

    wanted = targets.reshape(block_rows) - c * vocab_block
    matches = wanted[:, None] == jnp.arange(vocab_block, dtype=jnp.int32)[None, :]
    chosen = jnp.sum(jnp.where(matches, logits, 0.0), axis=-1)
    highest = jnp.max(logits, axis=-1)
    mass = jnp.sum(jnp.exp(logits - highest[:, None]), axis=-1)
    shares = all_conts(jnp.stack([highest, mass, chosen]))
    summit = jnp.max(shares[:, 0], axis=0)
    mass_all = jnp.sum(shares[:, 1] * jnp.exp(shares[:, 0] - summit), axis=0)
    token_logprob = (jnp.sum(shares[:, 2], axis=0) - (summit + jnp.log(mass_all))).reshape(targets.shape)
    path_score = jnp.mean(token_logprob, axis=-1)
    all_scores = everyone(path_score, ("tensor", "prefix")).reshape(-1)
    labels = jnp.arange(QUESTIONS, dtype=jnp.int32)
    member = (questions[:, 0][:, None] == labels[None, :]).astype(jnp.float32)
    question_score = jnp.sum(member * all_scores[:, None], axis=0) / jnp.sum(member, axis=0)
    return (
        context[None, None],
        hidden.reshape(path_count, SCORED, 1, sub_width),
        token_logprob,
        path_score,
        question_score,
    )


def solution(mesh):
    in_specs = (
        P("cont", None, "prefix"),
        P("prefix"),
        P(("prefix", "cont"), "tensor"),
        P(("prefix", "cont"), "tensor"),
        P(("prefix", "cont"), "tensor"),
        P("prefix", "cont", "tensor", None),
        P("prefix", "cont", "tensor", None),
        P("cont"),
        P("tensor", ("prefix", "cont")),
        P("prefix", "tensor"),
        P("prefix", "tensor", "cont"),
        P(("tensor", "prefix"), None),
        P(),
    )
    out_specs = (
        P("cont", "prefix", None, "tensor"),
        P("cont", None, "prefix", "tensor"),
        P(("tensor", "prefix"), None),
        P(("tensor", "prefix")),
        P(),
    )
    return jax.shard_map(body, mesh=mesh, in_specs=in_specs, out_specs=out_specs, check_vma=False)
```

time: 673 us -> 325 us (0.48)
  waiting for transfers between devices: 325 us -> 49.1 us
  blocking collectives: 279 us -> 173 us
  starting transfers between devices: 0.56 us -> 45.9 us
  matrix products: 30.9 us -> 7.51 us
    all_gather x4 -> x2, waiting for transfers between devices: 181 us -> 21 us  [the longest x1 21 us: body(): lax.all_gather(after(out_weight, weights), 'cont', axis_index_groups=bloc...]
    reduce_scatter x5 -> x0, waiting for transfers between devices: 143 us -> none  [the longest x1 100 us: body(): lax.psum_scatter(jnp.dot(every_row, head_block, preferred_element_type=jn...]
    psum x3 -> x0, blocking collectives: 141 us -> none  [the longest x1 68.5 us: body(): lax.psum(jnp.sum(member_local * path_score[:, None], axis=0), ('tensor',...]
    all_to_all x0 -> x6, blocking collectives: none -> 109 us  [the longest x5 95.3 us: everyone(): return lax.all_to_all(spread, axis, 0, 0, axis_index_groups=groups)]
    all_gather x6 -> x2, blocking collectives: 114 us -> 64.4 us  [body(): lax.all_gather(cache.reshape(-1, head_width), 'cont', axis=0, tiled=True)]
    ppermute x0 -> x9, starting transfers between devices: none -> 28.1 us  [the longest x2 7.9 us: choose(): beside = lax.ppermute(mine, 'prefix', first_perm)]
    unnamed x1 -> x0, blocking collectives: 24.1 us -> none
    dot_general x11 -> x3, matrix products: 30.9 us -> 7.51 us  [the longest x2 7.17 us: project(): full = jnp.dot(normed, weight, preferred_element_type=jnp.float32)]
  transfers between devices with their start and end apart: 9 -> 14, of which waited for: 6 -> 6; matrix products, arithmetic and copies ran while one was open for 6% -> 6% of each run, Pallas kernels for 0% -> 2%
where the time goes in v1:
time: 325 us; the launch traced here: 323 us
  blocking collectives  173 us (53%)
  waiting for transfers between devices  49.1 us (15%)
  starting transfers between devices  45.9 us (14%)
  between operations  17.8 us (5%)
  other arithmetic  15.4 us (5%)
  local copies, waits for them, and re-layouts  8.32 us (3%)
  matrix products  7.51 us (2%)
  Pallas kernels  6.1 us (2%)
    all_to_all x5, blocking collectives, everyone(): return lax.all_to_all(spread, axis, 0, 0, axis_index_groups=groups)  95.3 us
    all_gather x2, blocking collectives, body(): lax.all_gather(cache.reshape(-1, head_width), 'cont', axis=0, tiled=True)  64.4 us
    all_gather x1, waiting for transfers between devices, body(): lax.all_gather(after(out_weight, weights), 'cont', axis_index_groups=bloc...  21 us
    all_to_all x1, blocking collectives, body(): summed = jnp.sum(lax.all_to_all(pieces, 'tensor', 0, 0), axis=0)  13.4 us
    all_to_all x1, waiting for transfers between devices, body(): lax.all_to_all(payload.reshape(blocks, block_rows, vocab_block + lanes),...  12.4 us
    all_to_all x1, starting transfers between devices, body(): lax.all_to_all(payload.reshape(blocks, block_rows, vocab_block + lanes),...  9.5 us
    all_to_all x2, starting transfers between devices, everyone(): return lax.all_to_all(spread, axis, 0, 0, axis_index_groups=groups)  8.25 us
    ppermute x2, starting transfers between devices, choose(): beside = lax.ppermute(mine, 'prefix', first_perm)  7.9 us
  transfers between devices with their start and end apart: 14, of which 6 were waited for; matrix products, arithmetic and copies ran while one was open for 6% of the time, Pallas kernels for 2%

profile of v1, /device:TPU:1, one launch (start us, length us, event | category | flops | bytes accessed | tf_op | source)
XLA Modules:
  0.0 323.3 jit_solution(10976910752391768449)
XLA Ops:
  11.7 4.8 %all-to-all-start = ((f32[4,4,128]{2,1,0:T(4,128)}), f32[4,4,128]{2,1,0:T(4,128)S(1)}, u32[]{:S(2)}, u32[]{:S(2)}) async-start(f32[4,4,128]{2,1,0:T(4,128)} %broadcast_in_dim.60), calls=%async_computation | async-start | bytes 16384 | tf_op jit(solution)/shard_map/all_to_all | solution.py:109
  16.6 35.9 %all-gather.1 = bf16[1,2048,1,128]{3,1,2,0:T(8,128)(2,1)S(1)} all-gather(bf16[1,128,1,128]{3,1,2,0:T(8,128)(2,1)S(1)} %copy-done.7), channel_id=3, replica_groups=mesh['tensor'=8,'prefix'=4,'cont'=16] {'cont'}, dimensions={1}, use_global_device_ids=true | all-gather | bytes 557056 | tf_op jit(solution)/shard_map/all_gather | solution.py:147
  52.5 5.6 %collective-permute-start.6 = (bf16[2048,128]{1,0:T(8,128)(2,1)S(1)}, bf16[2048,128]{1,0:T(8,128)(2,1)}, u32[]{:S(2)}, u32[]{:S(2)}) collective-permute-start(bf16[2048,128]{1,0:T(8,128)(2,1)S(1)} %bitcast.73), channel_id=1, source_target_pairs={{0,48},{16,32},{32,16},{48,0},{1,49},{17,33},{33,17},{49,1},{2,50}... | collective-permute-start | bytes 1572872 | tf_op jit(solution)/shard_map/ppermute | solution.py:179
  58.1 28.5 %all-gather = bf16[1,2048,1,128]{3,1,2,0:T(8,128)(2,1)S(1)} all-gather(bf16[1,128,1,128]{3,1,2,0:T(8,128)(2,1)S(1)} %copy-done.8), channel_id=2, replica_groups=mesh['tensor'=8,'prefix'=4,'cont'=16] {'cont'}, dimensions={1}, use_global_device_ids=true | all-gather | bytes 557056 | tf_op jit(solution)/shard_map/all_gather | solution.py:147
  94.7 2.9 collective-permute-start.7
  98.5 3.5 %collective-permute-start.5 = (bf16[2048,128]{1,0:T(8,128)(2,1)}, bf16[2048,128]{1,0:T(8,128)(2,1)}, u32[]{:S(2)}, u32[]{:S(2)}) collective-permute-start(bf16[2048,128]{1,0:T(8,128)(2,1)} %broadcast_select_fusion.1), channel_id=1, source_target_pairs={{0,48},{16,32},{32,16},{48,0},{1,49},{17,33},{33,17},{49,1},{2,50}... | collective-permute-start | bytes 1572872 | tf_op jit(solution)/shard_map/ppermute | solution.py:181
  102.1 3.6 %fusion.4 = f32[4,128,640]{2,1,0:T(8,128)S(1)} fusion(bf16[2048,1280]{1,0:T(8,128)(2,1)} %all-gather.6.cloned.1.call-done, bf16[4,128,2048]{2,1,0:T(8,128)(2,1)S(1)} %copy-done.2, f32[2048]{0:T(1024)S(1)} %copy-done.15, f32[4,128]{1,0:T(4,128)S(1)} %add_rsqrt_fusion), kind=kOutput, calls=%fused_computation.8 | convolution fusion | flops 1346371584 | bytes 6039552 | tf_op jit(solution)/shard_map/dot_general | solution.py:166
  110.1 3.6 %fusion.3 = f32[4,128,640]{2,1,0:T(8,128)S(1)} fusion(bf16[2048,1280]{1,0:T(8,128)(2,1)} %all-gather.6.cloned.1.call-done, bf16[4,128,2048]{2,1,0:T(8,128)(2,1)S(1)} %copy-done.2, f32[2048]{0:T(1024)S(1)} %copy-done.15, f32[4,128]{1,0:T(4,128)S(1)} %add_rsqrt_fusion), kind=kOutput, calls=%fused_computation.6 | convolution fusion | flops 1346371584 | bytes 6039552 | tf_op jit(solution)/shard_map/dot_general | solution.py:166
  113.8 3.5 %collective-permute-start.2 = (f32[2,128,640]{2,1,0:T(8,128)S(1)}, f32[2,128,640]{2,1,0:T(8,128)S(1)}, u32[]{:S(2)}, u32[]{:S(2)}) collective-permute-start(f32[2,128,640]{2,1,0:T(8,128)S(1)} %pad_maximum_fusion.1), channel_id=1, source_target_pairs={{0,48},{16,32},{32,16},{48,0},{1,49},{17,33},{33,17},{49,1},{2,50}... | collective-permute-start | bytes 1966088 | tf_op jit(solution)/shard_map/ppermute | solution.py:191
  118.5 5.0 %collective-permute-done = f32[2,128,640]{2,1,0:T(8,128)} collective-permute-done((f32[2,128,640]{2,1,0:T(8,128)}, f32[2,128,640]{2,1,0:T(8,128)}, u32[]{:S(2)}, u32[]{:S(2)}) %collective-permute-start) | collective-permute-done | bytes 655392 | tf_op jit(solution)/shard_map/ppermute | solution.py:191
  124.5 4.1 %collective-permute-start.1 = (f32[128,640]{1,0:T(8,128)S(1)}, f32[128,640]{1,0:T(8,128)S(1)}, u32[]{:S(2)}, u32[]{:S(2)}) collective-permute-start(f32[128,640]{1,0:T(8,128)S(1)} %fusion.12), channel_id=1, source_target_pairs={{0,48},{16,32},{32,16},{48,0},{1,49},{17,33},{33,17},{49,1},{2,50}... | collective-permute-start | bytes 983048 | tf_op jit(solution)/shard_map/ppermute | solution.py:192
  130.9 3.2 collective-permute-start.3
  139.4 5.7 %shard_map.164 = bf16[128,1024]{1,0:T(8,128)(2,1)} custom-call(f32[128,1024]{1,0:T(8,128)S(1)} %pad_maximum_fusion.3.q_ref, f32[128,128]{1,0:T(8,128)S(1)} %get-tuple-element.29.cos_ref, f32[128,128]{1,0:T(8,128)S(1)} %get-tuple-element.20.sin_ref, bf16[128,128]{1,0:T(8,128)(2,1)S(1)} %get-tuple-element.19.kf_ref, bf16[128,128]{1,0:T(8,128)(2,1)S(1)} %slice.149.vf_ref, ...), custom_call_target="tpu_custom_call" | custom-call | flops 1140850688 | bytes 2097152 | tf_op jit(solution)/shard_map/pallas_call | solution.py:68
  145.8 25.2 %all_to_all.46 = bf16[8,8,1024]{2,1,0:T(8,128)(2,1)S(1)} all-to-all(bf16[8,8,1024]{2,1,0:T(8,128)(2,1)S(1)} %broadcast_in_dim.62), channel_id=1, replica_groups={{0,8,16,24,32,40,48,56},{1,9,17,25,33,41,49,57},{2,10,18,26,34,42,50,58..., dimensions={0} | all-to-all | bytes 262144 | tf_op jit(solution)/shard_map/all_to_all | solution.py:109
  171.0 21.0 %all-gather.8.cloned.1.call-done = bf16[8192,128]{1,0:T(8,128)(2,1)} async-done(((bf16[1024,128]{1,0:T(8,128)(2,1)}), bf16[8192,128]{1,0:T(8,128)(2,1)}) %all-gather.8.cloned.1.call-update) | async-done | bytes 2097168 | tf_op jit(solution)/shard_map/all_gather | solution.py:153
  194.0 13.4 %all_to_all.47 = f32[8,32,256]{2,1,0:T(8,128)S(1)} all-to-all(f32[8,32,256]{2,1,0:T(8,128)S(1)} %shard_map.165), channel_id=1, replica_groups=mesh['tensor'=8,'prefix'=4,'cont'=16] {'tensor'}, dimensions={0} | all-to-all | bytes 524288 | tf_op jit(solution)/shard_map/all_to_all | solution.py:223
  208.2 35.2 %all_to_all.48 = bf16[4,32,256]{2,1,0:T(8,128)(2,1)S(1)} all-to-all(bf16[4,32,256]{2,1,0:T(8,128)(2,1)S(1)} %broadcast_in_dim.63), channel_id=1, replica_groups={{0,4,8,12},{1,5,9,13},{2,6,10,14},{3,7,11,15},{16,20,24,28},{17,21,25,2..., dimensions={0} | all-to-all | bytes 131072 | tf_op jit(solution)/shard_map/all_to_all | solution.py:109
  244.1 3.4 %all-to-all-start.4 = ((bf16[4,4,32,256]{3,2,1,0:T(8,128)(2,1)}), bf16[4,4,32,256]{3,2,1,0:T(8,128)(2,1)S(1)}, u32[]{:S(2)}, u32[]{:S(2)}) async-start(bf16[4,4,32,256]{3,2,1,0:T(8,128)(2,1)} %broadcast_in_dim.64), calls=%async_computation.4 | async-start | bytes 524288 | tf_op jit(solution)/shard_map/all_to_all | solution.py:109
  247.5 5.6 %all-to-all-done.4 = bf16[4,4,32,256]{3,2,1,0:T(8,128)(2,1)S(1)} async-done(((bf16[4,4,32,256]{3,2,1,0:T(8,128)(2,1)}), bf16[4,4,32,256]{3,2,1,0:T(8,128)(2,1)S(1)}, u32[]{:S(2)}, u32[]{:S(2)}) %all-to-all-start.4) | async-done | bytes 262176 | tf_op jit(solution)/shard_map/all_to_all | solution.py:109
  255.0 9.5 %all-to-all-start.5 = ((bf16[32,16,640]{2,1,0:T(8,128)(2,1)}), bf16[32,16,640]{2,1,0:T(8,128)(2,1)S(1)}, u32[]{:S(2)}, u32[]{:S(2)}) async-start(bf16[32,16,640]{2,1,0:T(8,128)(2,1)} %bitcast.23), calls=%async_computation.5 | async-start | bytes 1310720 | tf_op jit(solution)/shard_map/all_to_all | solution.py:249
  264.6 12.4 %all-to-all-done.5 = bf16[32,16,640]{2,1,0:T(8,128)(2,1)S(1)} async-done(((bf16[32,16,640]{2,1,0:T(8,128)(2,1)}), bf16[32,16,640]{2,1,0:T(8,128)(2,1)S(1)}, u32[]{:S(2)}, u32[]{:S(2)}) %all-to-all-start.5) | async-done | bytes 655392 | tf_op jit(solution)/shard_map/all_to_all | solution.py:249
  277.8 13.7 %all_to_all.49 = f32[4,3,16]{2,1,0:T(4,128)S(1)} all-to-all(f32[4,3,16]{2,1,0:T(4,128)S(1)} %broadcast_in_dim.71), channel_id=1, replica_groups={{0,4,8,12},{1,5,9,13},{2,6,10,14},{3,7,11,15},{16,20,24,28},{17,21,25,2..., dimensions={0} | all-to-all | bytes 1536 | tf_op jit(solution)/shard_map/all_to_all | solution.py:109
  291.6 7.4 %all_to_all.50 = f32[4,1,192]{2,1,0:T(1,128)S(1)} all-to-all(f32[4,1,192]{2,1,0:T(1,128)S(1)} %reshape.159), channel_id=1, replica_groups={{0,1,2,3},{4,5,6,7},{8,9,10,11},{12,13,14,15},{16,17,18,19},{20,21,22,2..., dimensions={0} | all-to-all | bytes 6144 | tf_op jit(solution)/shard_map/all_to_all | solution.py:109
  300.6 13.9 %all_to_all.51 = f32[32,1,2]{2,1,0:T(1,128)S(1)} all-to-all(f32[32,1,2]{2,1,0:T(1,128)S(1)} %broadcast_in_dim.73), channel_id=1, replica_groups=mesh['tensor'=8,'prefix'=4,'cont'=16] {'tensor','prefix'}, dimensions={0} | all-to-all | bytes 512 | tf_op jit(solution)/shard_map/all_to_all | solution.py:109
  (121 shorter events, 34.8 us)
Async XLA Ops:
  7.2 246.2 %copy-start = (bf16[1,256,512]{2,1,0:T(8,128)(2,1)S(1)}, bf16[1,256,512]{2,1,0:T(8,128)(2,1)}, u32[]{:S(2)}) copy-start(bf16[1,256,512]{2,1,0:T(8,128)(2,1)} %param.23) | copy-start | bytes 786436
  7.2 50.9 %copy-start.8 = (bf16[1,128,1,128]{3,1,2,0:T(8,128)(2,1)S(1)}, bf16[1,128,1,128]{3,1,2,0:T(8,128)(2,1)}, u32[]{:S(2)}) copy-start(bf16[1,128,1,128]{3,1,2,0:T(8,128)(2,1)} %param.18) | copy-start | bytes 98308
  7.2 82.7 %copy-start.9 = (s32[4]{0:T(128)S(1)}, s32[4]{0:T(128)}, u32[]{:S(2)}) copy-start(s32[4]{0:T(128)} %param.20) | copy-start | bytes 52
  7.2 94.9 %all-gather.6.cloned.1.call-start = ((), (), s32[]{:S(2)}) async-start(), calls=%async_computation.9 | async-start | bytes 5570560 | tf_op jit(solution)/shard_map/all_gather | solution.py:146
  11.7 82.0 %all-to-all-start = ((f32[4,4,128]{2,1,0:T(4,128)}), f32[4,4,128]{2,1,0:T(4,128)S(1)}, u32[]{:S(2)}, u32[]{:S(2)}) async-start(f32[4,4,128]{2,1,0:T(4,128)} %broadcast_in_dim.60), calls=%async_computation | async-start | bytes 16384 | tf_op jit(solution)/shard_map/all_to_all | solution.py:109
  16.6 175.5 %all-gather.8.cloned.1.call-start = ((), (), s32[]{:S(2)}) async-start(), calls=%async_computation.10 | async-start | bytes 2359296 | tf_op jit(solution)/shard_map/all_gather | solution.py:153
  52.5 49.6 %copy-start.2 = (bf16[4,128,2048]{2,1,0:T(8,128)(2,1)S(1)}, bf16[4,128,2048]{2,1,0:T(8,128)(2,1)}, u32[]{:S(2)}) copy-start(bf16[4,128,2048]{2,1,0:T(8,128)(2,1)} %param.13) | copy-start | bytes 6291460
  52.5 41.3 %collective-permute-start.6 = (bf16[2048,128]{1,0:T(8,128)(2,1)S(1)}, bf16[2048,128]{1,0:T(8,128)(2,1)}, u32[]{:S(2)}, u32[]{:S(2)}) collective-permute-start(bf16[2048,128]{1,0:T(8,128)(2,1)S(1)} %bitcast.73), channel_id=1, source_target_pairs={{0,48},{16,32},{32,16},{48,0},{1,49},{17,33},{33,17},{49,1},{2,50}... | collective-permute-start | bytes 1572872 | tf_op jit(solution)/shard_map/ppermute | solution.py:179
  86.6 11.0 %collective-permute-start.4 = (bf16[2048,128]{1,0:T(8,128)(2,1)S(1)}, bf16[2048,128]{1,0:T(8,128)(2,1)}, u32[]{:S(2)}, u32[]{:S(2)}) collective-permute-start(bf16[2048,128]{1,0:T(8,128)(2,1)S(1)} %bitcast.72), channel_id=1, source_target_pairs={{0,16},{16,0},{32,48},{48,32},{1,17},{17,1},{33,49},{49,33},{2,18}... | collective-permute-start | bytes 1572872 | tf_op jit(solution)/shard_map/ppermute | solution.py:179
  94.7 22.7 %collective-permute-start.7 = (bf16[2048,128]{1,0:T(8,128)(2,1)}, bf16[2048,128]{1,0:T(8,128)(2,1)}, u32[]{:S(2)}, u32[]{:S(2)}) collective-permute-start(bf16[2048,128]{1,0:T(8,128)(2,1)} %broadcast_select_fusion), channel_id=1, source_target_pairs={{0,16},{16,0},{32,48},{48,32},{1,17},{17,1},{33,49},{49,33},{2,18}... | collective-permute-start | bytes 1572872 | tf_op jit(solution)/shard_map/ppermute | solution.py:181
  98.5 18.8 %collective-permute-start.5 = (bf16[2048,128]{1,0:T(8,128)(2,1)}, bf16[2048,128]{1,0:T(8,128)(2,1)}, u32[]{:S(2)}, u32[]{:S(2)}) collective-permute-start(bf16[2048,128]{1,0:T(8,128)(2,1)} %broadcast_select_fusion.1), channel_id=1, source_target_pairs={{0,48},{16,32},{32,16},{48,0},{1,49},{17,33},{33,17},{49,1},{2,50}... | collective-permute-start | bytes 1572872 | tf_op jit(solution)/shard_map/ppermute | solution.py:181
  107.8 15.8 %collective-permute-start = (f32[2,128,640]{2,1,0:T(8,128)}, f32[2,128,640]{2,1,0:T(8,128)}, u32[]{:S(2)}, u32[]{:S(2)}) collective-permute-start(f32[2,128,640]{2,1,0:T(8,128)} %pad_maximum_fusion), channel_id=1, source_target_pairs={{0,16},{16,0},{32,48},{48,32},{1,17},{17,1},{33,49},{49,33},{2,18}... | collective-permute-start | bytes 1966088 | tf_op jit(solution)/shard_map/ppermute | solution.py:191
  113.8 17.1 %collective-permute-start.2 = (f32[2,128,640]{2,1,0:T(8,128)S(1)}, f32[2,128,640]{2,1,0:T(8,128)S(1)}, u32[]{:S(2)}, u32[]{:S(2)}) collective-permute-start(f32[2,128,640]{2,1,0:T(8,128)S(1)} %pad_maximum_fusion.1), channel_id=1, source_target_pairs={{0,48},{16,32},{32,16},{48,0},{1,49},{17,33},{33,17},{49,1},{2,50}... | collective-permute-start | bytes 1966088 | tf_op jit(solution)/shard_map/ppermute | solution.py:191
  124.5 10.8 %collective-permute-start.1 = (f32[128,640]{1,0:T(8,128)S(1)}, f32[128,640]{1,0:T(8,128)S(1)}, u32[]{:S(2)}, u32[]{:S(2)}) collective-permute-start(f32[128,640]{1,0:T(8,128)S(1)} %fusion.12), channel_id=1, source_target_pairs={{0,48},{16,32},{32,16},{48,0},{1,49},{17,33},{33,17},{49,1},{2,50}... | collective-permute-start | bytes 983048 | tf_op jit(solution)/shard_map/ppermute | solution.py:192
  130.9 8.1 %collective-permute-start.3 = (f32[128,640]{1,0:T(8,128)S(1)}, f32[128,640]{1,0:T(8,128)S(1)}, u32[]{:S(2)}, u32[]{:S(2)}) collective-permute-start(f32[128,640]{1,0:T(8,128)S(1)} %fusion.9), channel_id=1, source_target_pairs={{0,16},{16,0},{32,48},{48,32},{1,17},{17,1},{33,49},{49,33},{2,18}... | collective-permute-start | bytes 983048 | tf_op jit(solution)/shard_map/ppermute | solution.py:192
  145.8 62.4 %slice-start = ((bf16[4,128,2048]{2,1,0:T(8,128)(2,1)}), bf16[4,8,2048]{2,1,0:T(8,128)(2,1)S(1)}, s32[]{:S(2)}) async-start(bf16[4,128,2048]{2,1,0:T(8,128)(2,1)} %param.13), calls=%async_computation.11 | async-start | bytes 262144 | tf_op jit(solution)/shard_map/slice | solution.py:233
  193.6 59.5 %copy-start.10 = (f32[1,256]{1,0:T(1,128)S(1)}, f32[1,256]{1,0:T(1,128)}, u32[]{:S(2)}) copy-start(f32[1,256]{1,0:T(1,128)} %param.22) | copy-start | bytes 3076
  207.5 0.7 collective-permute-start.8
  208.2 46.8 %copy-start.6 = (bf16[32,256]{1,0:T(8,128)(2,1)}, bf16[32,256]{1,0:T(8,128)(2,1)S(1)}, u32[]{:S(2)}) copy-start(bf16[32,256]{1,0:T(8,128)(2,1)S(1)} %fusion.18) | copy-start | bytes 49156
  244.1 9.0 %all-to-all-start.4 = ((bf16[4,4,32,256]{3,2,1,0:T(8,128)(2,1)}), bf16[4,4,32,256]{3,2,1,0:T(8,128)(2,1)S(1)}, u32[]{:S(2)}, u32[]{:S(2)}) async-start(bf16[4,4,32,256]{3,2,1,0:T(8,128)(2,1)} %broadcast_in_dim.64), calls=%async_computation.4 | async-start | bytes 524288 | tf_op jit(solution)/shard_map/all_to_all | solution.py:109
  253.9 61.8 %copy-start.14 = (s32[64,1]{0,1:T(1,128)S(1)}, s32[64,1]{0,1:T(1,128)}, u32[]{:S(2)}) copy-start(s32[64,1]{0,1:T(1,128)} %param.25) | copy-start | bytes 772
  255.0 22.0 %all-to-all-start.5 = ((bf16[32,16,640]{2,1,0:T(8,128)(2,1)}), bf16[32,16,640]{2,1,0:T(8,128)(2,1)S(1)}, u32[]{:S(2)}, u32[]{:S(2)}) async-start(bf16[32,16,640]{2,1,0:T(8,128)(2,1)} %bitcast.23), calls=%async_computation.5 | async-start | bytes 1310720 | tf_op jit(solution)/shard_map/all_to_all | solution.py:249
  300.4 16.0 %copy-start.12 = (f32[2,8]{1,0:T(2,128)}, f32[2,8]{1,0:T(2,128)S(1)}, u32[]{:S(2)}) copy-start(f32[2,8]{1,0:T(2,128)S(1)} %sub.57) | copy-start | bytes 196
  300.5 15.9 %copy-start.13 = (f32[2]{0:T(128)}, f32[2]{0:T(128)S(1)}, u32[]{:S(2)}) copy-start(f32[2]{0:T(128)S(1)} %broadcast_multiply_fusion) | copy-start | bytes 28
  (7 other events, 45.0 us)
Sparse Core Ops, SparseCore 0:
  10.1 88.9 all-gather.5
  110.2 81.7 all-gather.7

commit v2 on v1

--- a/solution.py
+++ b/solution.py
@@ -9,7 +9,6 @@
 
 SCORED = 8
 QUESTIONS = 8
-RESIDUES = 2
 
 epsilon = 1e-05
 rope_base = 500000.0
@@ -86,36 +85,13 @@
     )(q, cosine, sine, fresh_keys, fresh_values, keys, values)
 
 
-def output_kernel(rows_ref, weight_ref, out_ref):
-    pieces, cont_rows, _ = out_ref.shape
-    blocks, _, width = weight_ref.shape
-    spans = blocks // 2
-    rows = rows_ref[...]
-    for j in range(blocks):
-        product = jnp.dot(rows, weight_ref[j], preferred_element_type=jnp.float32)
-        for k in range(pieces // spans):
-            out_ref[k * spans + j // 2, :, (j % 2) * width : (j % 2 + 1) * width] = product[
-                k * cont_rows : (k + 1) * cont_rows
-            ]
-
-
 def after(array, earlier):
     return lax.optimization_barrier((array, earlier))[0]
 
 
-def everyone(array, axis, groups=None):
-    size = len(groups[0]) if groups else lax.axis_size(axis)
-    spread = jnp.broadcast_to(array[None], (size,) + array.shape)
-    return lax.all_to_all(spread, axis, 0, 0, axis_index_groups=groups)
-
-
-def all_conts(array):
-    size = lax.axis_size("cont")
-    side = math.isqrt(size)
-    strided = [[k + side * j for j in range(side)] for k in range(side)]
-    beside = [[side * j + k for k in range(side)] for j in range(side)]
-    found = everyone(everyone(array, "cont", strided), "cont", beside)
-    return jnp.swapaxes(found, 0, 1).reshape((size,) + array.shape)
+def everyone(array, axis):
+    size = lax.axis_size(axis)
+    return lax.all_to_all(jnp.broadcast_to(array[None], (size,) + array.shape), axis, 0, 0)
 
 
 def body(
@@ -142,20 +118,14 @@
     positions = prefix_span + jnp.arange(path_length, dtype=jnp.int32)
     cosine, sine = rope_tables(head_width, positions)
 
-    lead = jnp.concatenate([key_weight, value_weight, query_weight], 1)
-    weights = lax.all_gather(lead, "cont", axis=0, tiled=True)
+    lead = jnp.concatenate([out_weight.T, key_weight, value_weight, query_weight], 1)
+    gathered = lax.all_gather(lead, "cont", axis=0, tiled=True)
+    depth = out_weight.shape[0]
+    weights = gathered[:, depth:]
     gather_cache = lambda cache: lax.all_gather(
         cache.reshape(-1, head_width), "cont", axis=0, tiled=True
     )
     cached_keys, cached_values = gather_cache(prefix_keys), gather_cache(prefix_values)
-    near_conts = conts // RESIDUES
-    blocks_of = lambda size: [list(range(k, k + size)) for k in range(0, conts, size)]
-    window = lax.all_gather(
-        after(out_weight, weights),
-        "cont",
-        axis_index_groups=blocks_of(near_conts),
-    )
-
     inputs = states.astype(jnp.float32)
     squares = jnp.sum(everyone(jnp.sum(inputs * inputs, axis=-1), "prefix"), axis=0)
     scaling = lax.rsqrt(squares / full_width + epsilon)
@@ -199,41 +169,21 @@
     queries = jnp.concatenate([left[:, 2 * head_width :], right], 1)
     context = attend(queries, cosine, sine, fresh_keys, fresh_values, keys, values)
 
-    scored = context[path_length - SCORED :]
-    share = [
-        [q * conts + b + k * near_conts for q in range(prefixes) for k in range(RESIDUES)]
-        for b in range(near_conts)
-    ]
-    rows = everyone(scored, ("prefix", "cont"), share)
-    rows = rows.reshape(prefixes, RESIDUES, SCORED, -1).transpose(1, 0, 2, 3)
-    scored_rows = rows.reshape(RESIDUES * path_count * SCORED, -1)
     cont_rows = path_count * SCORED
+    scored_rows = everyone(context[path_length - SCORED :], "prefix").reshape(cont_rows, -1)
     sub_width = 2 * out_weight.shape[1]
-    spans = tensors // RESIDUES
-    pieces = pl.pallas_call(
-        output_kernel,
-        out_shape=jax.ShapeDtypeStruct((tensors, cont_rows, sub_width), jnp.float32),
-        compiler_params=pltpu.CompilerParams(vmem_limit_bytes=24 * 1024 * 1024),
-        cost_estimate=pl.CostEstimate(
-            flops=2 * scored_rows.size * window.shape[0] * window.shape[2],
-            bytes_accessed=2 * window.size,
-            transcendentals=0,
-        ),
-    )(scored_rows, window)
+    projected = lax.dot_general(
+        scored_rows,
+        gathered[:, :depth],
+        (((1,), (1,)), ((), ())),
+        preferred_element_type=jnp.float32,
+    )
+    pieces = projected.reshape(cont_rows, tensors, sub_width).transpose(1, 0, 2)
     summed = jnp.sum(lax.all_to_all(pieces, "tensor", 0, 0), axis=0)
-    perm = []
-    for k in range(RESIDUES):
-        for i in range(spans):
-            for a in range(RESIDUES):
-                for b in range(near_conts):
-                    here = (k * spans + i) * conts + a * near_conts + b
-                    perm.append((here, (a * spans + i) * conts + k * near_conts + b))
-    summed = lax.ppermute(summed, ("tensor", "cont"), perm)
-
     residual = lax.dynamic_slice_in_dim(states[:, path_length - SCORED :, :], t * sub_width, sub_width, 2)
     hidden = (summed + residual.reshape(cont_rows, sub_width).astype(jnp.float32)).astype(jnp.bfloat16)
 
-    every = all_conts(hidden).reshape(-1, sub_width).astype(jnp.float32)
+    every = lax.all_gather(hidden, "cont", axis=0, tiled=True).astype(jnp.float32)
     final_part = jnp.sum(every * every, axis=-1, keepdims=True)
     gained = (every * final_gain.reshape(sub_width)).astype(jnp.bfloat16)
     vocab_block = head_weight.shape[2]
@@ -258,7 +208,7 @@
     chosen = jnp.sum(jnp.where(matches, logits, 0.0), axis=-1)
     highest = jnp.max(logits, axis=-1)
     mass = jnp.sum(jnp.exp(logits - highest[:, None]), axis=-1)
-    shares = all_conts(jnp.stack([highest, mass, chosen]))
+    shares = everyone(jnp.stack([highest, mass, chosen]), "cont")
     summit = jnp.max(shares[:, 0], axis=0)
     mass_all = jnp.sum(shares[:, 1] * jnp.exp(shares[:, 0] - summit), axis=0)
     token_logprob = (jnp.sum(shares[:, 2], axis=0) - (summit + jnp.log(mass_all))).reshape(targets.shape)

time: 325 us -> 307 us (0.945)
  blocking collectives: 173 us -> 108 us
  waiting for transfers between devices: 49.1 us -> 77.8 us
  starting transfers between devices: 45.9 us -> 61.3 us
  matrix products: 7.51 us -> 11.7 us
  other arithmetic: 15.4 us -> 12 us
    all_to_all x6 -> x1, blocking collectives: 109 us -> 19.3 us  [everyone(): lax.all_to_all(jnp.broadcast_to(array[None], (size,) + array.shape), axis...]
    all_gather x0 -> x1, blocking collectives: none -> 21.6 us  [body(): lax.all_gather(hidden, 'cont', axis=0, tiled=True).astype(jnp.float32)]
    all_gather x2 -> x1, waiting for transfers between devices: 21 us -> 38.5 us  [body(): gathered = lax.all_gather(lead, 'cont', axis=0, tiled=True)]
    all_to_all x2 -> x4, starting transfers between devices: 8.25 us -> 23.3 us  [the longest x3 14.1 us: everyone(): lax.all_to_all(jnp.broadcast_to(array[None], (size,) + array.shape), axis...]
    all_to_all x2 -> x4, waiting for transfers between devices: 5.58 us -> 12.8 us  [the longest x1 6.47 us: body(): summed = jnp.sum(lax.all_to_all(pieces, 'tensor', 0, 0), axis=0)]
    slice x1 -> x3, local copies, waits for them, and re-layouts: 0.72 us -> 5.44 us  [the longest x1 4.7 us: body(): gathered[:, :depth]]
    dot_general x0 -> x1, matrix products: none -> 4.23 us  [body(): lax.dot_general(scored_rows, gathered[:, :depth], (((1,), (1,)), ((), ())...]
    ppermute x2, waiting for transfers between devices: 2.68 us -> 6.02 us  [path_sum(): passed = lax.ppermute(pick(second_p) + got[1], 'prefix', second_perm)]
  transfers between devices with their start and end apart: 14 -> 14, of which waited for: 6 -> 8; matrix products, arithmetic and copies ran while one was open for 6% -> 7% of each run, Pallas kernels for 2% -> 0%
where the time goes in v2:
time: 307 us; the launch traced here: 306 us
  blocking collectives  108 us (35%)
  waiting for transfers between devices  77.8 us (25%)
  starting transfers between devices  61.3 us (20%)
  between operations  17.8 us (6%)
  other arithmetic  12 us (4%)
  matrix products  11.7 us (4%)
  local copies, waits for them, and re-layouts  11.2 us (4%)
  Pallas kernels  5.67 us (2%)
    all_gather x2, blocking collectives, body(): lax.all_gather(cache.reshape(-1, head_width), 'cont', axis=0, tiled=True)  67.3 us
    all_gather x1, waiting for transfers between devices, body(): gathered = lax.all_gather(lead, 'cont', axis=0, tiled=True)  38.5 us
    all_gather x1, blocking collectives, body(): lax.all_gather(hidden, 'cont', axis=0, tiled=True).astype(jnp.float32)  21.6 us
    all_to_all x1, blocking collectives, everyone(): lax.all_to_all(jnp.broadcast_to(array[None], (size,) + array.shape), axis...  19.3 us
    all_to_all x3, starting transfers between devices, everyone(): lax.all_to_all(jnp.broadcast_to(array[None], (size,) + array.shape), axis...  14.1 us
    all_to_all x1, starting transfers between devices, body(): lax.all_to_all(payload.reshape(blocks, block_rows, vocab_block + lanes),...  12.6 us
    all_to_all x1, waiting for transfers between devices, body(): lax.all_to_all(payload.reshape(blocks, block_rows, vocab_block + lanes),...  12.4 us
    all_to_all x1, starting transfers between devices, body(): summed = jnp.sum(lax.all_to_all(pieces, 'tensor', 0, 0), axis=0)  9.2 us
  transfers between devices with their start and end apart: 14, of which 8 were waited for; matrix products, arithmetic and copies ran while one was open for 7% of the time, Pallas kernels for 0%

profile of v2, /device:TPU:1, one launch (start us, length us, event | category | flops | bytes accessed | tf_op | source)
XLA Modules:
  0.0 305.7 jit_solution(11487316811118958562)
XLA Ops:
  11.5 4.8 %all-to-all-start = ((f32[4,4,128]{2,1,0:T(4,128)}), f32[4,4,128]{2,1,0:T(4,128)S(1)}, u32[]{:S(2)}, u32[]{:S(2)}) async-start(f32[4,4,128]{2,1,0:T(4,128)} %broadcast_in_dim.54), calls=%async_computation | async-start | bytes 16384 | tf_op jit(solution)/shard_map/all_to_all | solution.py:94
  16.3 36.5 %all-gather.1 = bf16[1,2048,1,128]{3,1,2,0:T(8,128)(2,1)S(1)} all-gather(bf16[1,128,1,128]{3,1,2,0:T(8,128)(2,1)S(1)} %copy-done.3), channel_id=3, replica_groups=mesh['tensor'=8,'prefix'=4,'cont'=16] {'cont'}, dimensions={1}, use_global_device_ids=true | all-gather | bytes 557056 | tf_op jit(solution)/shard_map/all_gather | solution.py:125
  52.8 4.8 %collective-permute-start.6 = (bf16[2048,128]{1,0:T(8,128)(2,1)S(1)}, bf16[2048,128]{1,0:T(8,128)(2,1)}, u32[]{:S(2)}, u32[]{:S(2)}) collective-permute-start(bf16[2048,128]{1,0:T(8,128)(2,1)S(1)} %bitcast.66), channel_id=1, source_target_pairs={{0,48},{16,32},{32,16},{48,0},{1,49},{17,33},{33,17},{49,1},{2,50}... | collective-permute-start | bytes 1572872 | tf_op jit(solution)/shard_map/ppermute | solution.py:149
  57.6 30.7 %all-gather = bf16[1,2048,1,128]{3,1,2,0:T(8,128)(2,1)S(1)} all-gather(bf16[1,128,1,128]{3,1,2,0:T(8,128)(2,1)S(1)} %copy-done.4), channel_id=2, replica_groups=mesh['tensor'=8,'prefix'=4,'cont'=16] {'cont'}, dimensions={1}, use_global_device_ids=true | all-gather | bytes 557056 | tf_op jit(solution)/shard_map/all_gather | solution.py:125
  97.1 3.4 %collective-permute-start.7 = (bf16[2048,128]{1,0:T(8,128)(2,1)}, bf16[2048,128]{1,0:T(8,128)(2,1)}, u32[]{:S(2)}, u32[]{:S(2)}) collective-permute-start(bf16[2048,128]{1,0:T(8,128)(2,1)} %broadcast_select_fusion), channel_id=1, source_target_pairs={{0,16},{16,0},{32,48},{48,32},{1,17},{17,1},{33,49},{49,33},{2,18}... | collective-permute-start | bytes 1572872 | tf_op jit(solution)/shard_map/ppermute | solution.py:151
  103.2 38.5 %all-gather.4.cloned.1.call-done = bf16[2048,2304]{1,0:T(8,128)(2,1)} async-done(((bf16[128,2304]{1,0:T(8,128)(2,1)}), bf16[2048,2304]{1,0:T(8,128)(2,1)}) %all-gather.4.cloned.1.call-update) | async-done | bytes 9437200 | tf_op jit(solution)/shard_map/all_gather | solution.py:122
  141.7 3.6 %fusion.4 = f32[4,128,640]{2,1,0:T(8,128)S(1)} fusion(bf16[2048,2304]{1,0:T(8,128)(2,1)} %all-gather.4.cloned.1.call-done, bf16[4,128,2048]{2,1,0:T(8,128)(2,1)S(1)} %copy-done.1, f32[2048]{0:T(1024)S(1)} %copy-done.11, f32[4,128]{1,0:T(4,128)S(1)} %add_rsqrt_fusion), kind=kOutput, calls=%fused_computation.8 | convolution fusion | flops 1346371584 | bytes 6039552 | tf_op jit(solution)/shard_map/dot_general | solution.py:136
  148.7 3.6 %fusion.3 = f32[4,128,640]{2,1,0:T(8,128)S(1)} fusion(bf16[2048,2304]{1,0:T(8,128)(2,1)} %all-gather.4.cloned.1.call-done, bf16[4,128,2048]{2,1,0:T(8,128)(2,1)S(1)} %copy-done.1, f32[2048]{0:T(1024)S(1)} %copy-done.11, f32[4,128]{1,0:T(4,128)S(1)} %add_rsqrt_fusion), kind=kOutput, calls=%fused_computation.6 | convolution fusion | flops 1346371584 | bytes 6039552 | tf_op jit(solution)/shard_map/dot_general | solution.py:136
  152.4 3.7 %collective-permute-start.2 = (f32[2,128,640]{2,1,0:T(8,128)S(1)}, f32[2,128,640]{2,1,0:T(8,128)S(1)}, u32[]{:S(2)}, u32[]{:S(2)}) collective-permute-start(f32[2,128,640]{2,1,0:T(8,128)S(1)} %pad_maximum_fusion.1), channel_id=1, source_target_pairs={{0,48},{16,32},{32,16},{48,0},{1,49},{17,33},{33,17},{49,1},{2,50}... | collective-permute-start | bytes 1966088 | tf_op jit(solution)/shard_map/ppermute | solution.py:161
  157.3 5.9 %collective-permute-done = f32[2,128,640]{2,1,0:T(8,128)S(1)} collective-permute-done((f32[2,128,640]{2,1,0:T(8,128)S(1)}, f32[2,128,640]{2,1,0:T(8,128)S(1)}, u32[]{:S(2)}, u32[]{:S(2)}) %collective-permute-start) | collective-permute-done | bytes 655392 | tf_op jit(solution)/shard_map/ppermute | solution.py:161
  163.2 4.4 %collective-permute-start.1 = (f32[128,640]{1,0:T(8,128)S(1)}, f32[128,640]{1,0:T(8,128)S(1)}, u32[]{:S(2)}, u32[]{:S(2)}) collective-permute-start(f32[128,640]{1,0:T(8,128)S(1)} %fusion.12), channel_id=1, source_target_pairs={{0,48},{16,32},{32,16},{48,0},{1,49},{17,33},{33,17},{49,1},{2,50}... | collective-permute-start | bytes 983048 | tf_op jit(solution)/shard_map/ppermute | solution.py:162
  173.0 4.9 %collective-permute-done.1 = f32[128,640]{1,0:T(8,128)S(1)} collective-permute-done((f32[128,640]{1,0:T(8,128)S(1)}, f32[128,640]{1,0:T(8,128)S(1)}, u32[]{:S(2)}, u32[]{:S(2)}) %collective-permute-start.1) | collective-permute-done | bytes 327712 | tf_op jit(solution)/shard_map/ppermute | solution.py:162
  179.4 5.7 %shard_map.164 = bf16[128,1024]{1,0:T(8,128)(2,1)} custom-call(f32[128,1024]{1,0:T(8,128)S(1)} %pad_maximum_fusion.4.q_ref, f32[128,128]{1,0:T(8,128)S(1)} %get-tuple-element.23.cos_ref, f32[128,128]{1,0:T(8,128)S(1)} %get-tuple-element.16.sin_ref, bf16[128,128]{1,0:T(8,128)(2,1)S(1)} %get-tuple-element.15.kf_ref, bf16[128,128]{1,0:T(8,128)(2,1)S(1)} %slice.149.vf_ref, ...), custom_call_target="tpu_custom_call" | custom-call | flops 1140850688 | bytes 2097152 | tf_op jit(solution)/shard_map/pallas_call | solution.py:67
  186.5 3.3 %all-to-all-start.1 = ((bf16[4,8,1024]{2,1,0:T(8,128)(2,1)}), bf16[4,8,1024]{2,1,0:T(8,128)(2,1)S(1)}, u32[]{:S(2)}, u32[]{:S(2)}) async-start(bf16[4,8,1024]{2,1,0:T(8,128)(2,1)} %broadcast_in_dim.56), calls=%async_computation.1 | async-start | bytes 131072 | tf_op jit(solution)/shard_map/all_to_all | solution.py:94
  189.7 4.7 %slice.99 = bf16[2048,1024]{1,0:T(8,128)(2,1)} slice(bf16[2048,2304]{1,0:T(8,128)(2,1)} %all-gather.4.cloned.1.call-done), slice={[0:2048], [0:1024]} | slice | bytes 8388608 | tf_op jit(solution)/shard_map/slice | solution.py:177
  194.5 4.2 %convolution_bitcast_fusion = f32[8,32,256]{2,1,0:T(8,128)} fusion(bf16[8,256,1024]{2,1,0:T(8,128)(2,1)} %bitcast.64, bf16[4,8,1024]{2,1,0:T(8,128)(2,1)S(1)} %all-to-all-done.1), kind=kOutput, calls=%fused_computation.11 | convolution fusion | flops 134217728 | bytes 4521984 | tf_op jit(solution)/shard_map/dot_general | solution.py:175
  198.7 9.2 %all-to-all-start.2 = ((f32[8,32,256]{2,1,0:T(8,128)}), f32[8,32,256]{2,1,0:T(8,128)S(1)}, u32[]{:S(2)}, u32[]{:S(2)}) async-start(f32[8,32,256]{2,1,0:T(8,128)} %convolution_bitcast_fusion), calls=%async_computation.2 | async-start | bytes 524288 | tf_op jit(solution)/shard_map/all_to_all | solution.py:182
  207.9 6.5 %all-to-all-done.2 = f32[8,32,256]{2,1,0:T(8,128)S(1)} async-done(((f32[8,32,256]{2,1,0:T(8,128)}), f32[8,32,256]{2,1,0:T(8,128)S(1)}, u32[]{:S(2)}, u32[]{:S(2)}) %all-to-all-start.2) | async-done | bytes 262176 | tf_op jit(solution)/shard_map/all_to_all | solution.py:182
  214.4 21.6 %all_gather.15 = bf16[512,256]{1,0:T(8,128)(2,1)S(1)} all-gather(bf16[32,256]{1,0:T(8,128)(2,1)S(1)} %fusion.23), channel_id=1, replica_groups=mesh['tensor'=8,'prefix'=4,'cont'=16] {'cont'}, dimensions={0}, use_global_device_ids=true | all-gather | bytes 278528 | tf_op jit(solution)/shard_map/all_gather | solution.py:186
  237.8 12.6 %all-to-all-start.3 = ((bf16[32,16,640]{2,1,0:T(8,128)(2,1)}), bf16[32,16,640]{2,1,0:T(8,128)(2,1)S(1)}, u32[]{:S(2)}, u32[]{:S(2)}) async-start(bf16[32,16,640]{2,1,0:T(8,128)(2,1)} %bitcast.22), calls=%async_computation.3 | async-start | bytes 1310720 | tf_op jit(solution)/shard_map/all_to_all | solution.py:199
  250.5 12.4 %all-to-all-done.3 = bf16[32,16,640]{2,1,0:T(8,128)(2,1)S(1)} async-done(((bf16[32,16,640]{2,1,0:T(8,128)(2,1)}), bf16[32,16,640]{2,1,0:T(8,128)(2,1)S(1)}, u32[]{:S(2)}, u32[]{:S(2)}) %all-to-all-start.3) | async-done | bytes 655392 | tf_op jit(solution)/shard_map/all_to_all | solution.py:199
  263.6 19.3 %all_to_all.31 = f32[16,3,16]{2,1,0:T(4,128)S(1)} all-to-all(f32[16,3,16]{2,1,0:T(4,128)S(1)} %broadcast_in_dim.93), channel_id=1, replica_groups=mesh['tensor'=8,'prefix'=4,'cont'=16] {'cont'}, dimensions={0} | all-to-all | bytes 6144 | tf_op jit(solution)/shard_map/all_to_all | solution.py:94
  283.9 6.0 %all-to-all-start.5 = ((f32[32,1,2]{2,1,0:T(1,128)}), f32[32,1,2]{2,1,0:T(1,128)S(1)}, u32[]{:S(2)}, u32[]{:S(2)}) async-start(f32[32,1,2]{2,1,0:T(1,128)} %broadcast_in_dim.94), calls=%async_computation.5 | async-start | bytes 32768 | tf_op jit(solution)/shard_map/all_to_all | solution.py:94
  290.5 6.3 %all-to-all-done.5 = f32[32,1,2]{2,1,0:T(1,128)S(1)} async-done(((f32[32,1,2]{2,1,0:T(1,128)}), f32[32,1,2]{2,1,0:T(1,128)S(1)}, u32[]{:S(2)}, u32[]{:S(2)}) %all-to-all-start.5) | async-done | bytes 288 | tf_op jit(solution)/shard_map/all_to_all | solution.py:94
  (100 shorter events, 31.3 us)
Async XLA Ops:
  7.2 229.0 %copy-start = (bf16[1,256,512]{2,1,0:T(8,128)(2,1)S(1)}, bf16[1,256,512]{2,1,0:T(8,128)(2,1)}, u32[]{:S(2)}) copy-start(bf16[1,256,512]{2,1,0:T(8,128)(2,1)} %param.23) | copy-start | bytes 786436
  7.2 9.1 %copy-start.3 = (bf16[1,128,1,128]{3,1,2,0:T(8,128)(2,1)S(1)}, bf16[1,128,1,128]{3,1,2,0:T(8,128)(2,1)}, u32[]{:S(2)}) copy-start(bf16[1,128,1,128]{3,1,2,0:T(8,128)(2,1)} %param.19) | copy-start | bytes 98308
  7.2 134.5 %all-gather.4.cloned.1.call-start = ((), (), s32[]{:S(2)}) async-start(), calls=%async_computation.6 | async-start | bytes 10027008 | tf_op jit(solution)/shard_map/all_gather | solution.py:122
  8.5 49.1 %copy-start.4 = (bf16[1,128,1,128]{3,1,2,0:T(8,128)(2,1)S(1)}, bf16[1,128,1,128]{3,1,2,0:T(8,128)(2,1)}, u32[]{:S(2)}) copy-start(bf16[1,128,1,128]{3,1,2,0:T(8,128)(2,1)} %param.18) | copy-start | bytes 98308
  10.3 80.9 %copy-start.5 = (s32[4]{0:T(128)S(1)}, s32[4]{0:T(128)}, u32[]{:S(2)}) copy-start(s32[4]{0:T(128)} %param.20) | copy-start | bytes 52
  11.5 83.6 %all-to-all-start = ((f32[4,4,128]{2,1,0:T(4,128)}), f32[4,4,128]{2,1,0:T(4,128)S(1)}, u32[]{:S(2)}, u32[]{:S(2)}) async-start(f32[4,4,128]{2,1,0:T(4,128)} %broadcast_in_dim.54), calls=%async_computation | async-start | bytes 16384 | tf_op jit(solution)/shard_map/all_to_all | solution.py:94
  52.8 42.3 %collective-permute-start.6 = (bf16[2048,128]{1,0:T(8,128)(2,1)S(1)}, bf16[2048,128]{1,0:T(8,128)(2,1)}, u32[]{:S(2)}, u32[]{:S(2)}) collective-permute-start(bf16[2048,128]{1,0:T(8,128)(2,1)S(1)} %bitcast.66), channel_id=1, source_target_pairs={{0,48},{16,32},{32,16},{48,0},{1,49},{17,33},{33,17},{49,1},{2,50}... | collective-permute-start | bytes 1572872 | tf_op jit(solution)/shard_map/ppermute | solution.py:149
  88.3 12.1 %collective-permute-start.4 = (bf16[2048,128]{1,0:T(8,128)(2,1)S(1)}, bf16[2048,128]{1,0:T(8,128)(2,1)}, u32[]{:S(2)}, u32[]{:S(2)}) collective-permute-start(bf16[2048,128]{1,0:T(8,128)(2,1)S(1)} %bitcast.65), channel_id=1, source_target_pairs={{0,16},{16,0},{32,48},{48,32},{1,17},{17,1},{33,49},{49,33},{2,18}... | collective-permute-start | bytes 1572872 | tf_op jit(solution)/shard_map/ppermute | solution.py:149
  95.1 46.6 %copy-start.11 = (f32[2048]{0:T(1024)S(1)}, f32[2048]{0:T(1024)}, u32[]{:S(2)}) copy-start(f32[2048]{0:T(1024)} %param.14) | copy-start | bytes 24580
  97.1 59.0 %collective-permute-start.7 = (bf16[2048,128]{1,0:T(8,128)(2,1)}, bf16[2048,128]{1,0:T(8,128)(2,1)}, u32[]{:S(2)}, u32[]{:S(2)}) collective-permute-start(bf16[2048,128]{1,0:T(8,128)(2,1)} %broadcast_select_fusion), channel_id=1, source_target_pairs={{0,16},{16,0},{32,48},{48,32},{1,17},{17,1},{33,49},{49,33},{2,18}... | collective-permute-start | bytes 1572872 | tf_op jit(solution)/shard_map/ppermute | solution.py:151
  101.3 54.8 %collective-permute-start.5 = (bf16[2048,128]{1,0:T(8,128)(2,1)}, bf16[2048,128]{1,0:T(8,128)(2,1)}, u32[]{:S(2)}, u32[]{:S(2)}) collective-permute-start(bf16[2048,128]{1,0:T(8,128)(2,1)} %broadcast_select_fusion.1), channel_id=1, source_target_pairs={{0,48},{16,32},{32,16},{48,0},{1,49},{17,33},{33,17},{49,1},{2,50}... | collective-permute-start | bytes 1572872 | tf_op jit(solution)/shard_map/ppermute | solution.py:151
  145.4 17.7 %collective-permute-start = (f32[2,128,640]{2,1,0:T(8,128)S(1)}, f32[2,128,640]{2,1,0:T(8,128)S(1)}, u32[]{:S(2)}, u32[]{:S(2)}) collective-permute-start(f32[2,128,640]{2,1,0:T(8,128)S(1)} %pad_maximum_fusion), channel_id=1, source_target_pairs={{0,16},{16,0},{32,48},{48,32},{1,17},{17,1},{33,49},{49,33},{2,18}... | collective-permute-start | bytes 1966088 | tf_op jit(solution)/shard_map/ppermute | solution.py:161
  152.4 18.5 %collective-permute-start.2 = (f32[2,128,640]{2,1,0:T(8,128)S(1)}, f32[2,128,640]{2,1,0:T(8,128)S(1)}, u32[]{:S(2)}, u32[]{:S(2)}) collective-permute-start(f32[2,128,640]{2,1,0:T(8,128)S(1)} %pad_maximum_fusion.1), channel_id=1, source_target_pairs={{0,48},{16,32},{32,16},{48,0},{1,49},{17,33},{33,17},{49,1},{2,50}... | collective-permute-start | bytes 1966088 | tf_op jit(solution)/shard_map/ppermute | solution.py:161
  163.2 14.7 %collective-permute-start.1 = (f32[128,640]{1,0:T(8,128)S(1)}, f32[128,640]{1,0:T(8,128)S(1)}, u32[]{:S(2)}, u32[]{:S(2)}) collective-permute-start(f32[128,640]{1,0:T(8,128)S(1)} %fusion.12), channel_id=1, source_target_pairs={{0,48},{16,32},{32,16},{48,0},{1,49},{17,33},{33,17},{49,1},{2,50}... | collective-permute-start | bytes 983048 | tf_op jit(solution)/shard_map/ppermute | solution.py:162
  170.9 8.2 %collective-permute-start.3 = (f32[128,640]{1,0:T(8,128)S(1)}, f32[128,640]{1,0:T(8,128)S(1)}, u32[]{:S(2)}, u32[]{:S(2)}) collective-permute-start(f32[128,640]{1,0:T(8,128)S(1)} %fusion.9), channel_id=1, source_target_pairs={{0,16},{16,0},{32,48},{48,32},{1,17},{17,1},{33,49},{49,33},{2,18}... | collective-permute-start | bytes 983048 | tf_op jit(solution)/shard_map/ppermute | solution.py:162
  186.5 8.0 %all-to-all-start.1 = ((bf16[4,8,1024]{2,1,0:T(8,128)(2,1)}), bf16[4,8,1024]{2,1,0:T(8,128)(2,1)S(1)}, u32[]{:S(2)}, u32[]{:S(2)}) async-start(bf16[4,8,1024]{2,1,0:T(8,128)(2,1)} %broadcast_in_dim.56), calls=%async_computation.1 | async-start | bytes 131072 | tf_op jit(solution)/shard_map/all_to_all | solution.py:94
  194.4 41.8 %copy-start.6 = (f32[1,256]{1,0:T(1,128)S(1)}, f32[1,256]{1,0:T(1,128)}, u32[]{:S(2)}) copy-start(f32[1,256]{1,0:T(1,128)} %param.22) | copy-start | bytes 3076
  198.7 15.7 %all-to-all-start.2 = ((f32[8,32,256]{2,1,0:T(8,128)}), f32[8,32,256]{2,1,0:T(8,128)S(1)}, u32[]{:S(2)}, u32[]{:S(2)}) async-start(f32[8,32,256]{2,1,0:T(8,128)} %convolution_bitcast_fusion), calls=%async_computation.2 | async-start | bytes 524288 | tf_op jit(solution)/shard_map/all_to_all | solution.py:182
  236.6 13.8 %copy-start.7 = (s32[2,8]{1,0:T(2,128)S(1)}, s32[2,8]{1,0:T(2,128)}, u32[]{:S(2)}) copy-start(s32[2,8]{1,0:T(2,128)} %param.24) | copy-start | bytes 196
  236.7 61.4 %copy-start.10 = (s32[64,1]{0,1:T(1,128)S(1)}, s32[64,1]{0,1:T(1,128)}, u32[]{:S(2)}) copy-start(s32[64,1]{0,1:T(1,128)} %param.25) | copy-start | bytes 772
  237.8 25.1 %all-to-all-start.3 = ((bf16[32,16,640]{2,1,0:T(8,128)(2,1)}), bf16[32,16,640]{2,1,0:T(8,128)(2,1)S(1)}, u32[]{:S(2)}, u32[]{:S(2)}) async-start(bf16[32,16,640]{2,1,0:T(8,128)(2,1)} %bitcast.22), calls=%async_computation.3 | async-start | bytes 1310720 | tf_op jit(solution)/shard_map/all_to_all | solution.py:199
  283.1 15.7 %copy-start.8 = (f32[2,8]{1,0:T(2,128)}, f32[2,8]{1,0:T(2,128)S(1)}, u32[]{:S(2)}) copy-start(f32[2,8]{1,0:T(2,128)S(1)} %sub.57) | copy-start | bytes 196
  283.3 15.5 %copy-start.9 = (f32[2]{0:T(128)}, f32[2]{0:T(128)S(1)}, u32[]{:S(2)}) copy-start(f32[2]{0:T(128)S(1)} %broadcast_multiply_fusion) | copy-start | bytes 28
  283.9 12.9 %all-to-all-start.5 = ((f32[32,1,2]{2,1,0:T(1,128)}), f32[32,1,2]{2,1,0:T(1,128)S(1)}, u32[]{:S(2)}, u32[]{:S(2)}) async-start(f32[32,1,2]{2,1,0:T(1,128)} %broadcast_in_dim.94), calls=%async_computation.5 | async-start | bytes 32768 | tf_op jit(solution)/shard_map/all_to_all | solution.py:94
  (2 other events, 11.5 us)
Sparse Core Ops, SparseCore 0:
  10.5 131.2 all-gather.3

commit v3 on v2

--- a/solution.py
+++ b/solution.py
@@ -85,6 +85,15 @@
     )(q, cosine, sine, fresh_keys, fresh_values, keys, values)
 
 
+def output_kernel(rows_ref, weight_ref, out_ref):
+    blocks, _, width = weight_ref.shape
+    rows = rows_ref[...]
+    for j in range(blocks):
+        out_ref[j // 2, :, (j % 2) * width : (j % 2 + 1) * width] = jnp.dot(
+            rows, weight_ref[j], preferred_element_type=jnp.float32
+        )
+
+
 def after(array, earlier):
     return lax.optimization_barrier((array, earlier))[0]
 
@@ -118,14 +127,14 @@
     positions = prefix_span + jnp.arange(path_length, dtype=jnp.int32)
     cosine, sine = rope_tables(head_width, positions)
 
-    lead = jnp.concatenate([out_weight.T, key_weight, value_weight, query_weight], 1)
-    gathered = lax.all_gather(lead, "cont", axis=0, tiled=True)
-    depth = out_weight.shape[0]
-    weights = gathered[:, depth:]
+    lead = jnp.concatenate([key_weight, value_weight, query_weight], 1)
+    weights = lax.all_gather(lead, "cont", axis=0, tiled=True)
     gather_cache = lambda cache: lax.all_gather(
         cache.reshape(-1, head_width), "cont", axis=0, tiled=True
     )
     cached_keys, cached_values = gather_cache(prefix_keys), gather_cache(prefix_values)
+    window = lax.all_gather(after(out_weight, (weights, cached_keys, cached_values)), "cont")
+
     inputs = states.astype(jnp.float32)
     squares = jnp.sum(everyone(jnp.sum(inputs * inputs, axis=-1), "prefix"), axis=0)
     scaling = lax.rsqrt(squares / full_width + epsilon)
@@ -172,13 +181,16 @@
     cont_rows = path_count * SCORED
     scored_rows = everyone(context[path_length - SCORED :], "prefix").reshape(cont_rows, -1)
     sub_width = 2 * out_weight.shape[1]
-    projected = lax.dot_general(
-        scored_rows,
-        gathered[:, :depth],
-        (((1,), (1,)), ((), ())),
-        preferred_element_type=jnp.float32,
-    )
-    pieces = projected.reshape(cont_rows, tensors, sub_width).transpose(1, 0, 2)
+    pieces = pl.pallas_call(
+        output_kernel,
+        out_shape=jax.ShapeDtypeStruct((tensors, cont_rows, sub_width), jnp.float32),
+        compiler_params=pltpu.CompilerParams(vmem_limit_bytes=24 * 1024 * 1024),
+        cost_estimate=pl.CostEstimate(
+            flops=2 * scored_rows.size * window.shape[0] * window.shape[2],
+            bytes_accessed=2 * window.size,
+            transcendentals=0,
+        ),
+    )(scored_rows, window)
     summed = jnp.sum(lax.all_to_all(pieces, "tensor", 0, 0), axis=0)
     residual = lax.dynamic_slice_in_dim(states[:, path_length - SCORED :, :], t * sub_width, sub_width, 2)
     hidden = (summed + residual.reshape(cont_rows, sub_width).astype(jnp.float32)).astype(jnp.bfloat16)

time: 307 us -> 286 us (0.932)
  waiting for transfers between devices: 77.8 us -> 60 us
  blocking collectives: 108 us -> 114 us
  matrix products: 11.7 us -> 5.8 us
  local copies, waits for them, and re-layouts: 11.2 us -> 6.89 us
    all_gather x1 -> x2, waiting for transfers between devices: 38.5 us -> 24.6 us  [the longest x1 23.6 us: body(): weights = lax.all_gather(lead, 'cont', axis=0, tiled=True)]
    all_to_all x1 -> x2, blocking collectives: 19.3 us -> 25.9 us  [everyone(): lax.all_to_all(jnp.broadcast_to(array[None], (size,) + array.shape), axis...]
    all_to_all x3 -> x2, starting transfers between devices: 14.1 us -> 9.24 us  [everyone(): lax.all_to_all(jnp.broadcast_to(array[None], (size,) + array.shape), axis...]
    slice x1 -> x0, local copies, waits for them, and re-layouts: 4.7 us -> none  [body(): gathered[:, :depth]]
    all_to_all x1, starting transfers between devices: 9.2 us -> 13.8 us  [body(): summed = jnp.sum(lax.all_to_all(pieces, 'tensor', 0, 0), axis=0)]
    dot_general x1 -> x0, matrix products: 4.23 us -> none  [body(): lax.dot_general(scored_rows, gathered[:, :depth], (((1,), (1,)), ((), ())...]
    all_to_all x3 -> x2, waiting for transfers between devices: 6.3 us -> 6.31 us  [everyone(): lax.all_to_all(jnp.broadcast_to(array[None], (size,) + array.shape), axis...]
  transfers between devices with their start and end apart: 14 -> 14, of which waited for: 8 -> 7; matrix products, arithmetic and copies ran while one was open for 7% -> 4% of each run, Pallas kernels for 0% -> 2%
where the time goes in v3:
time: 286 us; the launch traced here: 285 us
  blocking collectives  114 us (40%)
  starting transfers between devices  63.6 us (22%)
  waiting for transfers between devices  60 us (21%)
  between operations  17.8 us (6%)
  other arithmetic  9.55 us (3%)
  Pallas kernels  7.05 us (2%)
  local copies, waits for them, and re-layouts  6.89 us (2%)
  matrix products  5.8 us (2%)
    all_gather x2, blocking collectives, body(): lax.all_gather(cache.reshape(-1, head_width), 'cont', axis=0, tiled=True)  64.7 us
    all_to_all x2, blocking collectives, everyone(): lax.all_to_all(jnp.broadcast_to(array[None], (size,) + array.shape), axis...  25.9 us
    all_gather x1, waiting for transfers between devices, body(): weights = lax.all_gather(lead, 'cont', axis=0, tiled=True)  23.6 us
    all_gather x1, blocking collectives, body(): lax.all_gather(hidden, 'cont', axis=0, tiled=True).astype(jnp.float32)  23.2 us
    all_to_all x1, starting transfers between devices, body(): summed = jnp.sum(lax.all_to_all(pieces, 'tensor', 0, 0), axis=0)  13.8 us
    all_to_all x1, starting transfers between devices, body(): lax.all_to_all(payload.reshape(blocks, block_rows, vocab_block + lanes),...  13 us
    all_to_all x1, waiting for transfers between devices, body(): lax.all_to_all(payload.reshape(blocks, block_rows, vocab_block + lanes),...  12.4 us
    all_to_all x2, starting transfers between devices, everyone(): lax.all_to_all(jnp.broadcast_to(array[None], (size,) + array.shape), axis...  9.24 us
  transfers between devices with their start and end apart: 14, of which 7 were waited for; matrix products, arithmetic and copies ran while one was open for 4% of the time, Pallas kernels for 2%

profile of v3, /device:TPU:1, one launch (start us, length us, event | category | flops | bytes accessed | tf_op | source)
XLA Modules:
  0.0 284.5 jit_solution(11569938752429905769)
XLA Ops:
  9.2 33.0 %all-gather.1 = bf16[1,2048,1,128]{3,1,2,0:T(8,128)(2,1)S(1)} all-gather(bf16[1,128,1,128]{3,1,2,0:T(8,128)(2,1)} %param.19), channel_id=3, replica_groups=mesh['tensor'=8,'prefix'=4,'cont'=16] {'cont'}, dimensions={1}, use_global_device_ids=true | all-gather | bytes 557056 | tf_op jit(solution)/shard_map/all_gather | solution.py:132
  42.2 31.7 %all-gather = bf16[1,2048,1,128]{3,1,2,0:T(8,128)(2,1)S(1)} all-gather(bf16[1,128,1,128]{3,1,2,0:T(8,128)(2,1)} %param.18), channel_id=2, replica_groups=mesh['tensor'=8,'prefix'=4,'cont'=16] {'cont'}, dimensions={1}, use_global_device_ids=true | all-gather | bytes 557056 | tf_op jit(solution)/shard_map/all_gather | solution.py:132
  73.9 23.6 %all-gather.6.cloned.1.call-done = bf16[2048,1280]{1,0:T(8,128)(2,1)} async-done(((bf16[128,1280]{1,0:T(8,128)(2,1)}), bf16[2048,1280]{1,0:T(8,128)(2,1)}) %all-gather.6.cloned.1.call-update) | async-done | bytes 5242896 | tf_op jit(solution)/shard_map/all_gather | solution.py:131
  97.5 3.8 %collective-permute-start.6 = (bf16[2048,128]{1,0:T(8,128)(2,1)S(1)}, bf16[2048,128]{1,0:T(8,128)(2,1)}, u32[]{:S(2)}, u32[]{:S(2)}) collective-permute-start(bf16[2048,128]{1,0:T(8,128)(2,1)S(1)} %bitcast.59), channel_id=1, source_target_pairs={{0,48},{16,32},{32,16},{48,0},{1,49},{17,33},{33,17},{49,1},{2,50}... | collective-permute-start | bytes 1572872 | tf_op jit(solution)/shard_map/ppermute | solution.py:158
  101.3 2.6 collective-permute-start.4
  105.1 3.2 %all-to-all-start = ((f32[4,4,128]{2,1,0:T(4,128)}), f32[4,4,128]{2,1,0:T(4,128)S(1)}, u32[]{:S(2)}, u32[]{:S(2)}) async-start(f32[4,4,128]{2,1,0:T(4,128)} %broadcast_in_dim.54), calls=%async_computation | async-start | bytes 16384 | tf_op jit(solution)/shard_map/all_to_all | solution.py:103
  113.3 3.3 %collective-permute-start.7 = (bf16[2048,128]{1,0:T(8,128)(2,1)S(1)}, bf16[2048,128]{1,0:T(8,128)(2,1)S(1)}, u32[]{:S(2)}, u32[]{:S(2)}) collective-permute-start(bf16[2048,128]{1,0:T(8,128)(2,1)S(1)} %broadcast_select_fusion), channel_id=1, source_target_pairs={{0,16},{16,0},{32,48},{48,32},{1,17},{17,1},{33,49},{49,33},{2,18}... | collective-permute-start | bytes 1572872 | tf_op jit(solution)/shard_map/ppermute | solution.py:160
  117.9 3.8 %collective-permute-start.5 = (bf16[2048,128]{1,0:T(8,128)(2,1)S(1)}, bf16[2048,128]{1,0:T(8,128)(2,1)S(1)}, u32[]{:S(2)}, u32[]{:S(2)}) collective-permute-start(bf16[2048,128]{1,0:T(8,128)(2,1)S(1)} %broadcast_select_fusion.1), channel_id=1, source_target_pairs={{0,48},{16,32},{32,16},{48,0},{1,49},{17,33},{33,17},{49,1},{2,50}... | collective-permute-start | bytes 1572872 | tf_op jit(solution)/shard_map/ppermute | solution.py:160
  121.7 3.6 %fusion.4 = f32[4,128,640]{2,1,0:T(8,128)S(1)} fusion(bf16[2048,1280]{1,0:T(8,128)(2,1)} %all-gather.6.cloned.1.call-done, bf16[4,128,2048]{2,1,0:T(8,128)(2,1)S(1)} %copy-done.2, f32[2048]{0:T(1024)S(1)} %copy-done.10, f32[4,128]{1,0:T(4,128)S(1)} %add_rsqrt_fusion), kind=kOutput, calls=%fused_computation.8 | convolution fusion | flops 1346371584 | bytes 6039552 | tf_op jit(solution)/shard_map/dot_general | solution.py:145
  129.6 2.6 collective-permute-start.2
  132.3 5.8 %collective-permute-done = f32[2,128,640]{2,1,0:T(8,128)S(1)} collective-permute-done((f32[2,128,640]{2,1,0:T(8,128)S(1)}, f32[2,128,640]{2,1,0:T(8,128)S(1)}, u32[]{:S(2)}, u32[]{:S(2)}) %collective-permute-start) | collective-permute-done | bytes 655392 | tf_op jit(solution)/shard_map/ppermute | solution.py:170
  138.1 6.3 %collective-permute-start.1 = (f32[128,640]{1,0:T(8,128)S(1)}, f32[128,640]{1,0:T(8,128)S(1)}, u32[]{:S(2)}, u32[]{:S(2)}) collective-permute-start(f32[128,640]{1,0:T(8,128)S(1)} %fusion.12), channel_id=1, source_target_pairs={{0,48},{16,32},{32,16},{48,0},{1,49},{17,33},{33,17},{49,1},{2,50}... | collective-permute-start | bytes 983048 | tf_op jit(solution)/shard_map/ppermute | solution.py:171
  144.5 2.8 collective-permute-start.3
  148.5 4.3 %collective-permute-done.1 = f32[128,640]{1,0:T(8,128)S(1)} collective-permute-done((f32[128,640]{1,0:T(8,128)S(1)}, f32[128,640]{1,0:T(8,128)S(1)}, u32[]{:S(2)}, u32[]{:S(2)}) %collective-permute-start.1) | collective-permute-done | bytes 327712 | tf_op jit(solution)/shard_map/ppermute | solution.py:171
  153.2 5.7 %shard_map.164 = bf16[128,1024]{1,0:T(8,128)(2,1)} custom-call(f32[128,1024]{1,0:T(8,128)S(1)} %pad_maximum_fusion.3.q_ref, f32[128,128]{1,0:T(8,128)S(1)} %get-tuple-element.25.cos_ref, f32[128,128]{1,0:T(8,128)S(1)} %get-tuple-element.18.sin_ref, bf16[128,128]{1,0:T(8,128)(2,1)S(1)} %get-tuple-element.17.kf_ref, bf16[128,128]{1,0:T(8,128)(2,1)S(1)} %slice.141.vf_ref, ...), custom_call_target="tpu_custom_call" | custom-call | flops 1140850688 | bytes 2097152 | tf_op jit(solution)/shard_map/pallas_call | solution.py:67
  159.6 8.2 %all_to_all.31 = bf16[4,8,1024]{2,1,0:T(8,128)(2,1)S(1)} all-to-all(bf16[4,8,1024]{2,1,0:T(8,128)(2,1)S(1)} %broadcast_in_dim.56), channel_id=1, replica_groups=mesh['tensor'=8,'prefix'=4,'cont'=16] {'prefix'}, dimensions={0} | all-to-all | bytes 131072 | tf_op jit(solution)/shard_map/all_to_all | solution.py:103
  172.5 13.8 %all-to-all-start.2 = ((f32[8,32,256]{2,1,0:T(8,128)}), f32[8,32,256]{2,1,0:T(8,128)S(1)}, u32[]{:S(2)}, u32[]{:S(2)}) async-start(f32[8,32,256]{2,1,0:T(8,128)} %shard_map.165), calls=%async_computation.2 | async-start | bytes 524288 | tf_op jit(solution)/shard_map/all_to_all | solution.py:194
  186.3 6.5 %all-to-all-done.2 = f32[8,32,256]{2,1,0:T(8,128)S(1)} async-done(((f32[8,32,256]{2,1,0:T(8,128)}), f32[8,32,256]{2,1,0:T(8,128)S(1)}, u32[]{:S(2)}, u32[]{:S(2)}) %all-to-all-start.2) | async-done | bytes 262176 | tf_op jit(solution)/shard_map/all_to_all | solution.py:194
  192.8 23.2 %all_gather.23 = bf16[512,256]{1,0:T(8,128)(2,1)S(1)} all-gather(bf16[32,256]{1,0:T(8,128)(2,1)S(1)} %fusion.22), channel_id=1, replica_groups=mesh['tensor'=8,'prefix'=4,'cont'=16] {'cont'}, dimensions={0}, use_global_device_ids=true | all-gather | bytes 278528 | tf_op jit(solution)/shard_map/all_gather | solution.py:198
  217.8 13.0 %all-to-all-start.3 = ((bf16[32,16,640]{2,1,0:T(8,128)(2,1)}), bf16[32,16,640]{2,1,0:T(8,128)(2,1)S(1)}, u32[]{:S(2)}, u32[]{:S(2)}) async-start(bf16[32,16,640]{2,1,0:T(8,128)(2,1)} %bitcast.19), calls=%async_computation.3 | async-start | bytes 1310720 | tf_op jit(solution)/shard_map/all_to_all | solution.py:211
  230.9 12.4 %all-to-all-done.3 = bf16[32,16,640]{2,1,0:T(8,128)(2,1)S(1)} async-done(((bf16[32,16,640]{2,1,0:T(8,128)(2,1)}), bf16[32,16,640]{2,1,0:T(8,128)(2,1)S(1)}, u32[]{:S(2)}, u32[]{:S(2)}) %all-to-all-start.3) | async-done | bytes 655392 | tf_op jit(solution)/shard_map/all_to_all | solution.py:211
  244.1 17.7 %all_to_all.32 = f32[16,3,16]{2,1,0:T(4,128)S(1)} all-to-all(f32[16,3,16]{2,1,0:T(4,128)S(1)} %broadcast_in_dim.93), channel_id=1, replica_groups=mesh['tensor'=8,'prefix'=4,'cont'=16] {'cont'}, dimensions={0} | all-to-all | bytes 6144 | tf_op jit(solution)/shard_map/all_to_all | solution.py:103
  262.8 6.0 %all-to-all-start.5 = ((f32[32,1,2]{2,1,0:T(1,128)}), f32[32,1,2]{2,1,0:T(1,128)S(1)}, u32[]{:S(2)}, u32[]{:S(2)}) async-start(f32[32,1,2]{2,1,0:T(1,128)} %broadcast_in_dim.94), calls=%async_computation.5 | async-start | bytes 32768 | tf_op jit(solution)/shard_map/all_to_all | solution.py:103
  269.4 6.3 %all-to-all-done.5 = f32[32,1,2]{2,1,0:T(1,128)S(1)} async-done(((f32[32,1,2]{2,1,0:T(1,128)}), f32[32,1,2]{2,1,0:T(1,128)S(1)}, u32[]{:S(2)}, u32[]{:S(2)}) %all-to-all-start.5) | async-done | bytes 288 | tf_op jit(solution)/shard_map/all_to_all | solution.py:103
  (103 shorter events, 23.4 us)
Async XLA Ops:
  7.2 209.0 %copy-start = (bf16[1,256,512]{2,1,0:T(8,128)(2,1)S(1)}, bf16[1,256,512]{2,1,0:T(8,128)(2,1)}, u32[]{:S(2)}) copy-start(bf16[1,256,512]{2,1,0:T(8,128)(2,1)} %param.23) | copy-start | bytes 786436
  7.2 96.8 %copy-start.2 = (bf16[4,128,2048]{2,1,0:T(8,128)(2,1)S(1)}, bf16[4,128,2048]{2,1,0:T(8,128)(2,1)}, u32[]{:S(2)}) copy-start(bf16[4,128,2048]{2,1,0:T(8,128)(2,1)} %param.13) | copy-start | bytes 6291460
  7.2 90.3 %all-gather.6.cloned.1.call-start = ((), (), s32[]{:S(2)}) async-start(), calls=%async_computation.6 | async-start | bytes 5570560 | tf_op jit(solution)/shard_map/all_gather | solution.py:131
  9.1 100.2 %copy-start.4 = (s32[4]{0:T(128)S(1)}, s32[4]{0:T(128)}, u32[]{:S(2)}) copy-start(s32[4]{0:T(128)} %param.20) | copy-start | bytes 52
  9.1 159.8 %all-gather.8.cloned.1.call-start = ((), (), s32[]{:S(2)}) async-start(), calls=%async_computation.7 | async-start | bytes 4456448 | tf_op jit(solution)/shard_map/all_gather | solution.py:136
  97.5 15.7 %collective-permute-start.6 = (bf16[2048,128]{1,0:T(8,128)(2,1)S(1)}, bf16[2048,128]{1,0:T(8,128)(2,1)}, u32[]{:S(2)}, u32[]{:S(2)}) collective-permute-start(bf16[2048,128]{1,0:T(8,128)(2,1)S(1)} %bitcast.59), channel_id=1, source_target_pairs={{0,48},{16,32},{32,16},{48,0},{1,49},{17,33},{33,17},{49,1},{2,50}... | collective-permute-start | bytes 1572872 | tf_op jit(solution)/shard_map/ppermute | solution.py:158
  101.3 15.3 %collective-permute-start.4 = (bf16[2048,128]{1,0:T(8,128)(2,1)S(1)}, bf16[2048,128]{1,0:T(8,128)(2,1)}, u32[]{:S(2)}, u32[]{:S(2)}) collective-permute-start(bf16[2048,128]{1,0:T(8,128)(2,1)S(1)} %bitcast.58), channel_id=1, source_target_pairs={{0,16},{16,0},{32,48},{48,32},{1,17},{17,1},{33,49},{49,33},{2,18}... | collective-permute-start | bytes 1572872 | tf_op jit(solution)/shard_map/ppermute | solution.py:158
  105.1 8.1 %all-to-all-start = ((f32[4,4,128]{2,1,0:T(4,128)}), f32[4,4,128]{2,1,0:T(4,128)S(1)}, u32[]{:S(2)}, u32[]{:S(2)}) async-start(f32[4,4,128]{2,1,0:T(4,128)} %broadcast_in_dim.54), calls=%async_computation | async-start | bytes 16384 | tf_op jit(solution)/shard_map/all_to_all | solution.py:103
  113.3 18.9 %collective-permute-start.7 = (bf16[2048,128]{1,0:T(8,128)(2,1)S(1)}, bf16[2048,128]{1,0:T(8,128)(2,1)S(1)}, u32[]{:S(2)}, u32[]{:S(2)}) collective-permute-start(bf16[2048,128]{1,0:T(8,128)(2,1)S(1)} %broadcast_select_fusion), channel_id=1, source_target_pairs={{0,16},{16,0},{32,48},{48,32},{1,17},{17,1},{33,49},{49,33},{2,18}... | collective-permute-start | bytes 1572872 | tf_op jit(solution)/shard_map/ppermute | solution.py:160
  116.6 11.0 %slice-start = ((s8[5242880]{0:T(1024)(128)(4,1)}), s8[4194304]{0:T(1024)(128)(4,1)S(1)}, s32[]{:S(2)}) async-start(s8[5242880]{0:T(1024)(128)(4,1)} %bitcast.70), calls=%async_computation.8 | async-start | bytes 8388608
  117.9 9.8 %slice-start.1 = ((s8[5242880]{0:T(1024)(128)(4,1)}), s8[1048576]{0:T(1024)(128)(4,1)S(1)}, s32[]{:S(2)}) async-start(s8[5242880]{0:T(1024)(128)(4,1)} %bitcast.70), calls=%async_computation.9 | async-start | bytes 2097152
  117.9 14.3 %collective-permute-start.5 = (bf16[2048,128]{1,0:T(8,128)(2,1)S(1)}, bf16[2048,128]{1,0:T(8,128)(2,1)S(1)}, u32[]{:S(2)}, u32[]{:S(2)}) collective-permute-start(bf16[2048,128]{1,0:T(8,128)(2,1)S(1)} %broadcast_select_fusion.1), channel_id=1, source_target_pairs={{0,48},{16,32},{32,16},{48,0},{1,49},{17,33},{33,17},{49,1},{2,50}... | collective-permute-start | bytes 1572872 | tf_op jit(solution)/shard_map/ppermute | solution.py:160
  125.5 12.6 %collective-permute-start = (f32[2,128,640]{2,1,0:T(8,128)S(1)}, f32[2,128,640]{2,1,0:T(8,128)S(1)}, u32[]{:S(2)}, u32[]{:S(2)}) collective-permute-start(f32[2,128,640]{2,1,0:T(8,128)S(1)} %pad_maximum_fusion), channel_id=1, source_target_pairs={{0,16},{16,0},{32,48},{48,32},{1,17},{17,1},{33,49},{49,33},{2,18}... | collective-permute-start | bytes 1966088 | tf_op jit(solution)/shard_map/ppermute | solution.py:170
  129.6 14.9 %collective-permute-start.2 = (f32[2,128,640]{2,1,0:T(8,128)S(1)}, f32[2,128,640]{2,1,0:T(8,128)S(1)}, u32[]{:S(2)}, u32[]{:S(2)}) collective-permute-start(f32[2,128,640]{2,1,0:T(8,128)S(1)} %pad_maximum_fusion.1), channel_id=1, source_target_pairs={{0,48},{16,32},{32,16},{48,0},{1,49},{17,33},{33,17},{49,1},{2,50}... | collective-permute-start | bytes 1966088 | tf_op jit(solution)/shard_map/ppermute | solution.py:170
  138.1 14.7 %collective-permute-start.1 = (f32[128,640]{1,0:T(8,128)S(1)}, f32[128,640]{1,0:T(8,128)S(1)}, u32[]{:S(2)}, u32[]{:S(2)}) collective-permute-start(f32[128,640]{1,0:T(8,128)S(1)} %fusion.12), channel_id=1, source_target_pairs={{0,48},{16,32},{32,16},{48,0},{1,49},{17,33},{33,17},{49,1},{2,50}... | collective-permute-start | bytes 983048 | tf_op jit(solution)/shard_map/ppermute | solution.py:171
  144.5 8.4 %collective-permute-start.3 = (f32[128,640]{1,0:T(8,128)S(1)}, f32[128,640]{1,0:T(8,128)S(1)}, u32[]{:S(2)}, u32[]{:S(2)}) collective-permute-start(f32[128,640]{1,0:T(8,128)S(1)} %fusion.9), channel_id=1, source_target_pairs={{0,16},{16,0},{32,48},{48,32},{1,17},{17,1},{33,49},{49,33},{2,18}... | collective-permute-start | bytes 983048 | tf_op jit(solution)/shard_map/ppermute | solution.py:171
  171.1 45.1 %copy-start.5 = (f32[1,256]{1,0:T(1,128)S(1)}, f32[1,256]{1,0:T(1,128)}, u32[]{:S(2)}) copy-start(f32[1,256]{1,0:T(1,128)} %param.22) | copy-start | bytes 3076
  172.5 20.3 %all-to-all-start.2 = ((f32[8,32,256]{2,1,0:T(8,128)}), f32[8,32,256]{2,1,0:T(8,128)S(1)}, u32[]{:S(2)}, u32[]{:S(2)}) async-start(f32[8,32,256]{2,1,0:T(8,128)} %shard_map.165), calls=%async_computation.2 | async-start | bytes 524288 | tf_op jit(solution)/shard_map/all_to_all | solution.py:194
  216.6 14.3 %copy-start.6 = (s32[2,8]{1,0:T(2,128)S(1)}, s32[2,8]{1,0:T(2,128)}, u32[]{:S(2)}) copy-start(s32[2,8]{1,0:T(2,128)} %param.24) | copy-start | bytes 196
  216.7 60.3 %copy-start.9 = (s32[64,1]{0,1:T(1,128)S(1)}, s32[64,1]{0,1:T(1,128)}, u32[]{:S(2)}) copy-start(s32[64,1]{0,1:T(1,128)} %param.25) | copy-start | bytes 772
  217.8 25.5 %all-to-all-start.3 = ((bf16[32,16,640]{2,1,0:T(8,128)(2,1)}), bf16[32,16,640]{2,1,0:T(8,128)(2,1)S(1)}, u32[]{:S(2)}, u32[]{:S(2)}) async-start(bf16[32,16,640]{2,1,0:T(8,128)(2,1)} %bitcast.19), calls=%async_computation.3 | async-start | bytes 1310720 | tf_op jit(solution)/shard_map/all_to_all | solution.py:211
  262.0 15.7 %copy-start.7 = (f32[2,8]{1,0:T(2,128)}, f32[2,8]{1,0:T(2,128)S(1)}, u32[]{:S(2)}) copy-start(f32[2,8]{1,0:T(2,128)S(1)} %sub.57) | copy-start | bytes 196
  262.2 15.6 %copy-start.8 = (f32[2]{0:T(128)}, f32[2]{0:T(128)S(1)}, u32[]{:S(2)}) copy-start(f32[2]{0:T(128)S(1)} %broadcast_multiply_fusion) | copy-start | bytes 28
  262.8 12.9 %all-to-all-start.5 = ((f32[32,1,2]{2,1,0:T(1,128)}), f32[32,1,2]{2,1,0:T(1,128)S(1)}, u32[]{:S(2)}, u32[]{:S(2)}) async-start(f32[32,1,2]{2,1,0:T(1,128)} %broadcast_in_dim.94), calls=%async_computation.5 | async-start | bytes 32768 | tf_op jit(solution)/shard_map/all_to_all | solution.py:103
  (3 other events, 15.3 us)
Sparse Core Ops, SparseCore 0:
  10.1 87.3 all-gather.5
  99.5 69.3 all-gather.7

commit v4 on v2

--- a/solution.py
+++ b/solution.py
@@ -32,20 +32,20 @@
 
 def attend_kernel(q_ref, cos_ref, sin_ref, kf_ref, vf_ref, kp_ref, vp_ref, out_ref):
     length, width = cos_ref.shape
+    fresh = kf_ref.shape[0]
     heads = q_ref.shape[1] // width
     cosine, sine = cos_ref[...], sin_ref[...]
     turned = []
     for h in range(heads):
         q = q_ref[:, h * width : (h + 1) * width]
-        turned.append((q * cosine + pltpu.roll(q, width // 2, 1) * sine).astype(jnp.bfloat16))
-    queries = jnp.concatenate(turned, 0)
+        turned.append(q * cosine + pltpu.roll(q, width // 2, 1) * sine)
+    queries = jnp.concatenate(turned, 0).astype(jnp.bfloat16)
     contract = (((1,), (1,)), ((), ()))
     old = lax.dot_general(queries, kp_ref[...], contract, preferred_element_type=jnp.float32)
     new = lax.dot_general(queries, kf_ref[...], contract, preferred_element_type=jnp.float32)
-    row = lax.broadcasted_iota(jnp.int32, (length, length), 0)
-    column = lax.broadcasted_iota(jnp.int32, (length, length), 1)
-    allowed = jnp.concatenate([column <= row] * heads, 0)
-    new = jnp.where(allowed, new, far_below)
+    row = lax.rem(lax.broadcasted_iota(jnp.int32, new.shape, 0), length) + (fresh - length)
+    column = lax.broadcasted_iota(jnp.int32, new.shape, 1)
+    new = jnp.where(column <= row, new, far_below)
     peak = jnp.maximum(jnp.max(old, -1, keepdims=True), jnp.max(new, -1, keepdims=True))
     factor = math.log2(math.e) / math.sqrt(width)
     old = jnp.exp2((old - peak) * factor)
@@ -53,22 +53,22 @@
     total = jnp.sum(old, -1, keepdims=True) + jnp.sum(new, -1, keepdims=True)
     mixed = jnp.dot(old.astype(jnp.bfloat16), vp_ref[...], preferred_element_type=jnp.float32)
     mixed += jnp.dot(new.astype(jnp.bfloat16), vf_ref[...], preferred_element_type=jnp.float32)
-    mixed = (mixed / total).astype(jnp.bfloat16)
+    mixed = (mixed / total).astype(out_ref.dtype)
     for h in range(heads):
         out_ref[:, h * width : (h + 1) * width] = mixed[h * length : (h + 1) * length]
 
 
-def attend(q, cosine, sine, fresh_keys, fresh_values, keys, values):
+def attend(q, cosine, sine, fresh_keys, fresh_values, keys, values, heads, out_type):
     length, columns = q.shape
     width = cosine.shape[1]
-    pair = 2 * width
+    step = heads * width
     whole = lambda array: pl.BlockSpec(array.shape, lambda i: (0, 0))
-    count = (columns // width) * length * (keys.shape[0] + length)
+    count = (columns // width) * length * (keys.shape[0] + fresh_keys.shape[0])
     return pl.pallas_call(
         attend_kernel,
-        grid=(columns // pair,),
+        grid=(columns // step,),
         in_specs=[
-            pl.BlockSpec((length, pair), lambda i: (0, i)),
+            pl.BlockSpec((length, step), lambda i: (0, i)),
             whole(cosine),
             whole(sine),
             whole(fresh_keys),
@@ -76,8 +76,8 @@
             whole(keys),
             whole(values),
         ],
-        out_specs=pl.BlockSpec((length, pair), lambda i: (0, i)),
-        out_shape=jax.ShapeDtypeStruct((length, columns), jnp.bfloat16),
+        out_specs=pl.BlockSpec((length, step), lambda i: (0, i)),
+        out_shape=jax.ShapeDtypeStruct((length, columns), out_type),
         compiler_params=pltpu.CompilerParams(vmem_limit_bytes=40 * 1024 * 1024),
         cost_estimate=pl.CostEstimate(
             flops=4 * count * width, bytes_accessed=2 * 1024 * 1024, transcendentals=count
@@ -132,9 +132,9 @@
     normed = (inputs * scaling[..., None] * norm_gain).astype(jnp.bfloat16)
     normed = normed.reshape(path_count * path_length, width_block)
 
-    def project(weight):
-        full = jnp.dot(normed, weight, preferred_element_type=jnp.float32)
-        return full.reshape(path_count, path_length, -1)
+    def project(rows, weight):
+        full = jnp.dot(rows, weight, preferred_element_type=jnp.float32)
+        return full.reshape(path_count, -1, weight.shape[1])
 
     owner_of = lambda q: lax.dynamic_index_in_dim(path_prefix, q, 0, keepdims=False)
     owner = owner_of(p)
@@ -142,14 +142,14 @@
     far = [(i, prefixes - 1 - i) for i in range(prefixes)]
     near_p, far_p = p ^ 1, prefixes - 1 - p
 
-    middle = weights.shape[1] // 2
-    left_part, right_part = project(weights[:, :middle]), project(weights[:, middle:])
+    fresh_columns = 2 * head_width
+    fresh_part = project(normed, weights[:, :fresh_columns])
 
     def choose(mine, first_perm, first_p, second_perm, second_p):
         beside = lax.ppermute(mine, "prefix", first_perm)
         sent = jnp.where(owner_of(second_p) == first_p, beside, mine)
         across = lax.ppermute(sent, "prefix", second_perm)
-        across = after(across, left_part)
+        across = after(across, fresh_part)
         return jnp.where(owner == p, mine, jnp.where(owner == first_p, beside, across))
 
     keys = choose(cached_keys, near, near_p, far, far_p)
@@ -162,19 +162,43 @@
         passed = lax.ppermute(pick(second_p) + got[1], "prefix", second_perm)
         return pick(p) + got[0] + passed
 
-    left = path_sum(left_part, near, near_p, far, far_p)
-    right = path_sum(right_part, far, far_p, near, near_p)
-    fresh_keys = rotate(left[:, :head_width], cosine, sine).astype(jnp.bfloat16)
-    fresh_values = left[:, head_width : 2 * head_width].astype(jnp.bfloat16)
-    queries = jnp.concatenate([left[:, 2 * head_width :], right], 1)
-    context = attend(queries, cosine, sine, fresh_keys, fresh_values, keys, values)
+    query_columns = weights.shape[1] - fresh_columns
+    scored_normed = normed.reshape(path_count, path_length, -1)[:, path_length - SCORED :]
+    scored_part = project(scored_normed.reshape(path_count * SCORED, -1), weights[:, fresh_columns:])
+    scored_part = lax.optimization_barrier(scored_part)
+    chunks = query_columns // fresh_columns
+    scored_part = scored_part.reshape(path_count, SCORED, chunks, fresh_columns)
+    scored_part = scored_part.transpose(0, 2, 1, 3).reshape(path_count, -1, fresh_columns)
+    early = jnp.concatenate([fresh_part, scored_part], 1)
+    early = jnp.sum(lax.all_to_all(early, "prefix", 0, 0), axis=0)
+    fresh_keys = rotate(early[:path_length, :head_width], cosine, sine).astype(jnp.bfloat16)
+    fresh_values = early[:path_length, head_width:].astype(jnp.bfloat16)
+    scored_queries = early[path_length:].reshape(chunks, SCORED, fresh_columns)
+    scored_queries = scored_queries.transpose(1, 0, 2).reshape(SCORED, query_columns)
+    scored_context = attend(
+        scored_queries,
+        cosine[path_length - SCORED :],
+        sine[path_length - SCORED :],
+        fresh_keys,
+        fresh_values,
+        keys,
+        values,
+        query_columns // head_width,
+        jnp.float32,
+    ).astype(jnp.bfloat16)
+
+    rows_later = after(normed, scored_context)
+    middle = fresh_columns + query_columns // 2
+    left = path_sum(project(rows_later, weights[:, fresh_columns:middle]), near, near_p, far, far_p)
+    right = path_sum(project(rows_later, weights[:, middle:]), far, far_p, near, near_p)
+    queries = jnp.concatenate([left, right], 1)
 
     cont_rows = path_count * SCORED
-    scored_rows = everyone(context[path_length - SCORED :], "prefix").reshape(cont_rows, -1)
+    scored_rows = everyone(scored_context, "prefix").reshape(cont_rows, -1)
     sub_width = 2 * out_weight.shape[1]
     projected = lax.dot_general(
         scored_rows,
-        gathered[:, :depth],
+        after(gathered, scored_context)[:, :depth],
         (((1,), (1,)), ((), ())),
         preferred_element_type=jnp.float32,
     )
@@ -196,10 +220,21 @@
     payload = jnp.concatenate([partial.astype(jnp.bfloat16), extra], 1)
     blocks = tensors * prefixes
     block_rows = targets.shape[0] * targets.shape[1]
+    context = attend(
+        after(queries, payload),
+        cosine,
+        sine,
+        fresh_keys,
+        fresh_values,
+        keys,
+        values,
+        2,
+        jnp.bfloat16,
+    )
     received = lax.all_to_all(
         payload.reshape(blocks, block_rows, vocab_block + lanes), ("tensor", "prefix"), 0, 0
     )
-    received = jnp.sum(received.astype(jnp.float32), axis=0)
+    received = jnp.sum(after(received, context).astype(jnp.float32), axis=0)
     final_sum = received[:, vocab_block] + received[:, vocab_block + 1]
     logits = received[:, :vocab_block] * lax.rsqrt(final_sum / full_width + epsilon)[:, None]
 

time: 307 us -> 303 us (0.987)
  waiting for transfers between devices: 77.8 us -> 50.7 us
  other arithmetic: 12 us -> 24.6 us
  matrix products: 11.7 us -> 16.8 us
  local copies, waits for them, and re-layouts: 11.2 us -> 15.4 us
    ppermute x2, waiting for transfers between devices: 8.05 us -> 0.01 us  [path_sum(): lax.ppermute(jnp.stack([pick(first_p), pick(third_p)]), 'prefix', first_p...]
    all_to_all x1, waiting for transfers between devices: 12.4 us -> 4.58 us  [body(): lax.all_to_all(payload.reshape(blocks, block_rows, vocab_block + lanes),...]
    all_to_all x0 -> x1, waiting for transfers between devices: none -> 7.78 us  [body(): early = jnp.sum(lax.all_to_all(early, 'prefix', 0, 0), axis=0)]
    all_gather x1, waiting for transfers between devices: 38.5 us -> 31.7 us  [body(): gathered = lax.all_gather(lead, 'cont', axis=0, tiled=True)]
    ppermute x2, waiting for transfers between devices: 6.02 us -> 0.01 us  [path_sum(): passed = lax.ppermute(pick(second_p) + got[1], 'prefix', second_perm)]
    all_to_all x1, waiting for transfers between devices: 6.47 us -> 1.04 us  [body(): summed = jnp.sum(lax.all_to_all(pieces, 'tensor', 0, 0), axis=0)]
    dot_general x3 -> x5, matrix products: 11.4 us -> 16.4 us  [the longest x4 12.2 us: project(): full = jnp.dot(rows, weight, preferred_element_type=jnp.float32)]
    all_to_all x0 -> x1, starting transfers between devices: none -> 4.13 us  [body(): early = jnp.sum(lax.all_to_all(early, 'prefix', 0, 0), axis=0)]
  transfers between devices with their start and end apart: 14 -> 15, of which waited for: 8 -> 5; matrix products, arithmetic and copies ran while one was open for 7% -> 15% of each run, Pallas kernels for 0% -> 2%
where the time goes in v4:
time: 303 us; the launch traced here: 302 us
  blocking collectives  108 us (36%)
  starting transfers between devices  62.3 us (21%)
  waiting for transfers between devices  50.7 us (17%)
  other arithmetic  24.6 us (8%)
  between operations  17.7 us (6%)
  matrix products  16.8 us (6%)
  local copies, waits for them, and re-layouts  15.4 us (5%)
  Pallas kernels  6.4 us (2%)
    all_gather x2, blocking collectives, body(): lax.all_gather(cache.reshape(-1, head_width), 'cont', axis=0, tiled=True)  66.5 us
    all_gather x1, waiting for transfers between devices, body(): gathered = lax.all_gather(lead, 'cont', axis=0, tiled=True)  31.7 us
    all_gather x1, blocking collectives, body(): lax.all_gather(hidden, 'cont', axis=0, tiled=True).astype(jnp.float32)  22.1 us
    all_to_all x1, blocking collectives, everyone(): lax.all_to_all(jnp.broadcast_to(array[None], (size,) + array.shape), axis...  19.2 us
    all_to_all x3, starting transfers between devices, everyone(): lax.all_to_all(jnp.broadcast_to(array[None], (size,) + array.shape), axis...  14.1 us
    dot_general x4, matrix products, project(): full = jnp.dot(rows, weight, preferred_element_type=jnp.float32)  12.2 us
    all_to_all x1, starting transfers between devices, body(): lax.all_to_all(payload.reshape(blocks, block_rows, vocab_block + lanes),...  11.3 us
    all_to_all x1, waiting for transfers between devices, body(): early = jnp.sum(lax.all_to_all(early, 'prefix', 0, 0), axis=0)  7.78 us
  transfers between devices with their start and end apart: 15, of which 5 were waited for; matrix products, arithmetic and copies ran while one was open for 15% of the time, Pallas kernels for 2%

profile of v4, /device:TPU:1, one launch (start us, length us, event | category | flops | bytes accessed | tf_op | source)
XLA Modules:
  0.0 301.7 jit_solution(4876650946227254608)
XLA Ops:
  11.5 4.8 %all-to-all-start = ((f32[4,4,128]{2,1,0:T(4,128)}), f32[4,4,128]{2,1,0:T(4,128)S(1)}, u32[]{:S(2)}, u32[]{:S(2)}) async-start(f32[4,4,128]{2,1,0:T(4,128)} %broadcast_in_dim.54), calls=%async_computation | async-start | bytes 16384 | tf_op jit(solution)/shard_map/all_to_all | solution.py:94
  16.3 36.5 %all-gather = bf16[1,2048,1,128]{3,1,2,0:T(8,128)(2,1)S(1)} all-gather(bf16[1,128,1,128]{3,1,2,0:T(8,128)(2,1)S(1)} %copy-done.6), channel_id=2, replica_groups=mesh['tensor'=8,'prefix'=4,'cont'=16] {'cont'}, dimensions={1}, use_global_device_ids=true | all-gather | bytes 557056 | tf_op jit(solution)/shard_map/all_gather | solution.py:125
  52.8 3.8 %collective-permute-start = (bf16[2048,128]{1,0:T(8,128)(2,1)S(1)}, bf16[2048,128]{1,0:T(8,128)(2,1)}, u32[]{:S(2)}, u32[]{:S(2)}) collective-permute-start(bf16[2048,128]{1,0:T(8,128)(2,1)S(1)} %bitcast.82), channel_id=1, source_target_pairs={{0,16},{16,0},{32,48},{48,32},{1,17},{17,1},{33,49},{49,33},{2,18}... | collective-permute-start | bytes 1572872 | tf_op jit(solution)/shard_map/ppermute | solution.py:149
  56.6 30.0 %all-gather.1 = bf16[1,2048,1,128]{3,1,2,0:T(8,128)(2,1)S(1)} all-gather(bf16[1,128,1,128]{3,1,2,0:T(8,128)(2,1)S(1)} %copy-done.7), channel_id=3, replica_groups=mesh['tensor'=8,'prefix'=4,'cont'=16] {'cont'}, dimensions={1}, use_global_device_ids=true | all-gather | bytes 557056 | tf_op jit(solution)/shard_map/all_gather | solution.py:125
  103.4 3.8 %collective-permute-start.1 = (bf16[2048,128]{1,0:T(8,128)(2,1)}, bf16[2048,128]{1,0:T(8,128)(2,1)}, u32[]{:S(2)}, u32[]{:S(2)}) collective-permute-start(bf16[2048,128]{1,0:T(8,128)(2,1)} %broadcast_select_fusion.1), channel_id=1, source_target_pairs={{0,48},{16,32},{32,16},{48,0},{1,49},{17,33},{33,17},{49,1},{2,50}... | collective-permute-start | bytes 1572872 | tf_op jit(solution)/shard_map/ppermute | solution.py:151
  110.0 31.7 %all-gather.4.cloned.1.call-done = bf16[2048,2304]{1,0:T(8,128)(2,1)} async-done(((bf16[128,2304]{1,0:T(8,128)(2,1)}), bf16[2048,2304]{1,0:T(8,128)(2,1)}) %all-gather.4.cloned.1.call-update) | async-done | bytes 9437200 | tf_op jit(solution)/shard_map/all_gather | solution.py:122
  141.7 3.0 fusion.3
  147.5 4.1 %all-to-all-start.1 = ((f32[4,160,256]{2,1,0:T(8,128)}), f32[4,160,256]{2,1,0:T(8,128)S(1)}, u32[]{:S(2)}, u32[]{:S(2)}) async-start(f32[4,160,256]{2,1,0:T(8,128)} %pad_maximum_fusion), calls=%async_computation.1 | async-start | bytes 1310720 | tf_op jit(solution)/shard_map/all_to_all | solution.py:173
  154.0 7.8 %all-to-all-done.1 = f32[4,160,256]{2,1,0:T(8,128)S(1)} async-done(((f32[4,160,256]{2,1,0:T(8,128)}), f32[4,160,256]{2,1,0:T(8,128)S(1)}, u32[]{:S(2)}, u32[]{:S(2)}) %all-to-all-start.1) | async-done | bytes 655392 | tf_op jit(solution)/shard_map/all_to_all | solution.py:173
  169.8 3.3 %all-to-all-start.2 = ((bf16[4,8,1024]{2,1,0:T(8,128)(2,1)}), bf16[4,8,1024]{2,1,0:T(8,128)(2,1)S(1)}, u32[]{:S(2)}, u32[]{:S(2)}) async-start(bf16[4,8,1024]{2,1,0:T(8,128)(2,1)} %broadcast_in_dim.55), calls=%async_computation.2 | async-start | bytes 131072 | tf_op jit(solution)/shard_map/all_to_all | solution.py:94
  173.1 4.4 %fusion.6 = f32[512,512]{1,0:T(8,128)} fusion(bf16[512,2048]{1,0:T(8,128)(2,1)} %bitcast.84, bf16[2048,2304]{1,0:T(8,128)(2,1)} %all-gather.4.cloned.1.call-done), kind=kOutput, calls=%fused_computation.9 | convolution fusion | flops 1073741824 | bytes 5242880 | tf_op jit(solution)/shard_map/dot_general | solution.py:136
  177.5 4.7 %slice.97 = bf16[2048,1024]{1,0:T(8,128)(2,1)} slice(bf16[2048,2304]{1,0:T(8,128)(2,1)} %all-gather.4.cloned.1.call-done), slice={[0:2048], [0:1024]} | slice | bytes 8388608 | tf_op jit(solution)/shard_map/slice | solution.py:201
  182.2 4.2 %convolution_bitcast_fusion = f32[8,32,256]{2,1,0:T(8,128)} fusion(bf16[8,256,1024]{2,1,0:T(8,128)(2,1)} %bitcast.81, bf16[4,8,1024]{2,1,0:T(8,128)(2,1)S(1)} %all-to-all-done.2), kind=kOutput, calls=%fused_computation.13 | convolution fusion | flops 134217728 | bytes 4521984 | tf_op jit(solution)/shard_map/dot_general | solution.py:199
  186.5 6.4 %all-to-all-start.3 = ((f32[8,32,256]{2,1,0:T(8,128)}), f32[8,32,256]{2,1,0:T(8,128)S(1)}, u32[]{:S(2)}, u32[]{:S(2)}) async-start(f32[8,32,256]{2,1,0:T(8,128)} %convolution_bitcast_fusion), calls=%async_computation.3 | async-start | bytes 524288 | tf_op jit(solution)/shard_map/all_to_all | solution.py:206
  194.8 3.6 %collective-permute-start.4 = (f32[2,128,512]{2,1,0:T(8,128)}, f32[2,128,512]{2,1,0:T(8,128)}, u32[]{:S(2)}, u32[]{:S(2)}) collective-permute-start(f32[2,128,512]{2,1,0:T(8,128)} %pad_maximum_fusion.3), channel_id=1, source_target_pairs={{0,16},{16,0},{32,48},{48,32},{1,17},{17,1},{33,49},{49,33},{2,18}... | collective-permute-start | bytes 1572872 | tf_op jit(solution)/shard_map/ppermute | solution.py:161
  200.2 22.1 %all_gather.15 = bf16[512,256]{1,0:T(8,128)(2,1)S(1)} all-gather(bf16[32,256]{1,0:T(8,128)(2,1)S(1)} %fusion.25), channel_id=1, replica_groups=mesh['tensor'=8,'prefix'=4,'cont'=16] {'cont'}, dimensions={0}, use_global_device_ids=true | all-gather | bytes 278528 | tf_op jit(solution)/shard_map/all_gather | solution.py:210
  224.7 3.9 %collective-permute-start.7 = (f32[128,512]{1,0:T(8,128)}, f32[128,512]{1,0:T(8,128)}, u32[]{:S(2)}, u32[]{:S(2)}) collective-permute-start(f32[128,512]{1,0:T(8,128)} %fusion.12), channel_id=1, source_target_pairs={{0,16},{16,0},{32,48},{48,32},{1,17},{17,1},{33,49},{49,33},{2,18}... | collective-permute-start | bytes 786440 | tf_op jit(solution)/shard_map/ppermute | solution.py:162
  230.3 3.7 %collective-permute-start.5 = (f32[128,512]{1,0:T(8,128)}, f32[128,512]{1,0:T(8,128)}, u32[]{:S(2)}, u32[]{:S(2)}) collective-permute-start(f32[128,512]{1,0:T(8,128)} %fusion.15), channel_id=1, source_target_pairs={{0,48},{16,32},{32,16},{48,0},{1,49},{17,33},{33,17},{49,1},{2,50}... | collective-permute-start | bytes 786440 | tf_op jit(solution)/shard_map/ppermute | solution.py:162
  235.1 11.3 %all-to-all-start.4 = ((bf16[32,16,640]{2,1,0:T(8,128)(2,1)}), bf16[32,16,640]{2,1,0:T(8,128)(2,1)S(1)}, u32[]{:S(2)}, u32[]{:S(2)}) async-start(bf16[32,16,640]{2,1,0:T(8,128)(2,1)} %bitcast.31), calls=%async_computation.4 | async-start | bytes 1310720 | tf_op jit(solution)/shard_map/all_to_all | solution.py:234
  248.8 5.7 %shard_map.165 = bf16[128,1024]{1,0:T(8,128)(2,1)} custom-call(f32[128,1024]{1,0:T(8,128)S(1)} %pad_maximum_fusion.5.q_ref, f32[128,128]{1,0:T(8,128)S(1)} %get-tuple-element.31.cos_ref, f32[128,128]{1,0:T(8,128)S(1)} %get-tuple-element.24.sin_ref, bf16[128,128]{1,0:T(8,128)(2,1)S(1)} %get-tuple-element.23.kf_ref, bf16[128,128]{1,0:T(8,128)(2,1)S(1)} %slice.190.vf_ref, ...), custom_call_target="tpu_custom_call" | custom-call | flops 1140850688 | bytes 2097152 | tf_op jit(solution)/shard_map/pallas_call | solution.py:67
  254.5 4.6 %all-to-all-done.4 = bf16[32,16,640]{2,1,0:T(8,128)(2,1)S(1)} async-done(((bf16[32,16,640]{2,1,0:T(8,128)(2,1)}), bf16[32,16,640]{2,1,0:T(8,128)(2,1)S(1)}, u32[]{:S(2)}, u32[]{:S(2)}) %all-to-all-start.4) | async-done | bytes 655392 | tf_op jit(solution)/shard_map/all_to_all | solution.py:234
  259.8 19.2 %all_to_all.36 = f32[16,3,16]{2,1,0:T(4,128)S(1)} all-to-all(f32[16,3,16]{2,1,0:T(4,128)S(1)} %broadcast_in_dim.93), channel_id=1, replica_groups=mesh['tensor'=8,'prefix'=4,'cont'=16] {'cont'}, dimensions={0} | all-to-all | bytes 6144 | tf_op jit(solution)/shard_map/all_to_all | solution.py:94
  279.9 6.0 %all-to-all-start.6 = ((f32[32,1,2]{2,1,0:T(1,128)}), f32[32,1,2]{2,1,0:T(1,128)S(1)}, u32[]{:S(2)}, u32[]{:S(2)}) async-start(f32[32,1,2]{2,1,0:T(1,128)} %broadcast_in_dim.94), calls=%async_computation.6 | async-start | bytes 32768 | tf_op jit(solution)/shard_map/all_to_all | solution.py:94
  287.3 5.6 %all-to-all-done.6 = f32[32,1,2]{2,1,0:T(1,128)S(1)} async-done(((f32[32,1,2]{2,1,0:T(1,128)}), f32[32,1,2]{2,1,0:T(1,128)S(1)}, u32[]{:S(2)}, u32[]{:S(2)}) %all-to-all-start.6) | async-done | bytes 288 | tf_op jit(solution)/shard_map/all_to_all | solution.py:94
  (115 shorter events, 49.7 us)
Async XLA Ops:
  7.2 215.4 %copy-start = (bf16[1,256,512]{2,1,0:T(8,128)(2,1)S(1)}, bf16[1,256,512]{2,1,0:T(8,128)(2,1)}, u32[]{:S(2)}) copy-start(bf16[1,256,512]{2,1,0:T(8,128)(2,1)} %param.23) | copy-start | bytes 786436
  7.2 134.5 %all-gather.4.cloned.1.call-start = ((), (), s32[]{:S(2)}) async-start(), calls=%async_computation.7 | async-start | bytes 10027008 | tf_op jit(solution)/shard_map/all_gather | solution.py:122
  8.5 48.1 %copy-start.7 = (bf16[1,128,1,128]{3,1,2,0:T(8,128)(2,1)S(1)}, bf16[1,128,1,128]{3,1,2,0:T(8,128)(2,1)}, u32[]{:S(2)}) copy-start(bf16[1,128,1,128]{3,1,2,0:T(8,128)(2,1)} %param.19) | copy-start | bytes 98308
  11.5 87.3 %all-to-all-start = ((f32[4,4,128]{2,1,0:T(4,128)}), f32[4,4,128]{2,1,0:T(4,128)S(1)}, u32[]{:S(2)}, u32[]{:S(2)}) async-start(f32[4,4,128]{2,1,0:T(4,128)} %broadcast_in_dim.54), calls=%async_computation | async-start | bytes 16384 | tf_op jit(solution)/shard_map/all_to_all | solution.py:94
  52.8 49.7 %collective-permute-start = (bf16[2048,128]{1,0:T(8,128)(2,1)S(1)}, bf16[2048,128]{1,0:T(8,128)(2,1)}, u32[]{:S(2)}, u32[]{:S(2)}) collective-permute-start(bf16[2048,128]{1,0:T(8,128)(2,1)S(1)} %bitcast.82), channel_id=1, source_target_pairs={{0,16},{16,0},{32,48},{48,32},{1,17},{17,1},{33,49},{49,33},{2,18}... | collective-permute-start | bytes 1572872 | tf_op jit(solution)/shard_map/ppermute | solution.py:149
  86.6 20.6 %collective-permute-start.2 = (bf16[2048,128]{1,0:T(8,128)(2,1)S(1)}, bf16[2048,128]{1,0:T(8,128)(2,1)}, u32[]{:S(2)}, u32[]{:S(2)}) collective-permute-start(bf16[2048,128]{1,0:T(8,128)(2,1)S(1)} %bitcast.83), channel_id=1, source_target_pairs={{0,48},{16,32},{32,16},{48,0},{1,49},{17,33},{33,17},{49,1},{2,50}... | collective-permute-start | bytes 1572872 | tf_op jit(solution)/shard_map/ppermute | solution.py:149
  102.6 39.2 %copy-start.2 = (bf16[4,128,2048]{2,1,0:T(8,128)(2,1)S(1)}, bf16[4,128,2048]{2,1,0:T(8,128)(2,1)}, u32[]{:S(2)}) copy-start(bf16[4,128,2048]{2,1,0:T(8,128)(2,1)} %fusion.2) | copy-start | bytes 6291460
  103.4 48.3 %collective-permute-start.1 = (bf16[2048,128]{1,0:T(8,128)(2,1)}, bf16[2048,128]{1,0:T(8,128)(2,1)}, u32[]{:S(2)}, u32[]{:S(2)}) collective-permute-start(bf16[2048,128]{1,0:T(8,128)(2,1)} %broadcast_select_fusion.1), channel_id=1, source_target_pairs={{0,48},{16,32},{32,16},{48,0},{1,49},{17,33},{33,17},{49,1},{2,50}... | collective-permute-start | bytes 1572872 | tf_op jit(solution)/shard_map/ppermute | solution.py:151
  108.1 43.6 %collective-permute-start.3 = (bf16[2048,128]{1,0:T(8,128)(2,1)}, bf16[2048,128]{1,0:T(8,128)(2,1)}, u32[]{:S(2)}, u32[]{:S(2)}) collective-permute-start(bf16[2048,128]{1,0:T(8,128)(2,1)} %broadcast_select_fusion), channel_id=1, source_target_pairs={{0,16},{16,0},{32,48},{48,32},{1,17},{17,1},{33,49},{49,33},{2,18}... | collective-permute-start | bytes 1572872 | tf_op jit(solution)/shard_map/ppermute | solution.py:151
  147.5 14.2 %all-to-all-start.1 = ((f32[4,160,256]{2,1,0:T(8,128)}), f32[4,160,256]{2,1,0:T(8,128)S(1)}, u32[]{:S(2)}, u32[]{:S(2)}) async-start(f32[4,160,256]{2,1,0:T(8,128)} %pad_maximum_fusion), calls=%async_computation.1 | async-start | bytes 1310720 | tf_op jit(solution)/shard_map/all_to_all | solution.py:173
  166.4 56.6 %collective-permute-start.6 = (f32[2,128,512]{2,1,0:T(8,128)S(1)}, f32[2,128,512]{2,1,0:T(8,128)}, u32[]{:S(2)}, u32[]{:S(2)}) collective-permute-start(f32[2,128,512]{2,1,0:T(8,128)S(1)} %pad_maximum_fusion.4), channel_id=1, source_target_pairs={{0,48},{16,32},{32,16},{48,0},{1,49},{17,33},{33,17},{49,1},{2,50}... | collective-permute-start | bytes 1572872 | tf_op jit(solution)/shard_map/ppermute | solution.py:161
  169.8 12.4 %all-to-all-start.2 = ((bf16[4,8,1024]{2,1,0:T(8,128)(2,1)}), bf16[4,8,1024]{2,1,0:T(8,128)(2,1)S(1)}, u32[]{:S(2)}, u32[]{:S(2)}) async-start(bf16[4,8,1024]{2,1,0:T(8,128)(2,1)} %broadcast_in_dim.55), calls=%async_computation.2 | async-start | bytes 131072 | tf_op jit(solution)/shard_map/all_to_all | solution.py:94
  186.5 36.0 %copy-start.11 = (pred[128]{0:T(512)(128)(4,1)S(1)}, pred[128]{0:T(512)(128)(4,1)}, u32[]{:S(2)}) copy-start(pred[128]{0:T(512)(128)(4,1)} %get-tuple-element.43) | copy-start | bytes 388
  186.5 36.0 %copy-start.12 = (pred[128]{0:T(512)(128)(4,1)S(1)}, pred[128]{0:T(512)(128)(4,1)}, u32[]{:S(2)}) copy-start(pred[128]{0:T(512)(128)(4,1)} %get-tuple-element.44) | copy-start | bytes 388
  186.5 36.1 %copy-start.8 = (f32[1,256]{1,0:T(1,128)S(1)}, f32[1,256]{1,0:T(1,128)}, u32[]{:S(2)}) copy-start(f32[1,256]{1,0:T(1,128)} %param.22) | copy-start | bytes 3076
  186.5 12.9 %all-to-all-start.3 = ((f32[8,32,256]{2,1,0:T(8,128)}), f32[8,32,256]{2,1,0:T(8,128)S(1)}, u32[]{:S(2)}, u32[]{:S(2)}) async-start(f32[8,32,256]{2,1,0:T(8,128)} %convolution_bitcast_fusion), calls=%async_computation.3 | async-start | bytes 524288 | tf_op jit(solution)/shard_map/all_to_all | solution.py:206
  194.8 33.7 %collective-permute-start.4 = (f32[2,128,512]{2,1,0:T(8,128)}, f32[2,128,512]{2,1,0:T(8,128)}, u32[]{:S(2)}, u32[]{:S(2)}) collective-permute-start(f32[2,128,512]{2,1,0:T(8,128)} %pad_maximum_fusion.3), channel_id=1, source_target_pairs={{0,16},{16,0},{32,48},{48,32},{1,17},{17,1},{33,49},{49,33},{2,18}... | collective-permute-start | bytes 1572872 | tf_op jit(solution)/shard_map/ppermute | solution.py:161
  224.7 21.8 %collective-permute-start.7 = (f32[128,512]{1,0:T(8,128)}, f32[128,512]{1,0:T(8,128)}, u32[]{:S(2)}, u32[]{:S(2)}) collective-permute-start(f32[128,512]{1,0:T(8,128)} %fusion.12), channel_id=1, source_target_pairs={{0,16},{16,0},{32,48},{48,32},{1,17},{17,1},{33,49},{49,33},{2,18}... | collective-permute-start | bytes 786440 | tf_op jit(solution)/shard_map/ppermute | solution.py:162
  230.3 17.3 %collective-permute-start.5 = (f32[128,512]{1,0:T(8,128)}, f32[128,512]{1,0:T(8,128)}, u32[]{:S(2)}, u32[]{:S(2)}) collective-permute-start(f32[128,512]{1,0:T(8,128)} %fusion.15), channel_id=1, source_target_pairs={{0,48},{16,32},{32,16},{48,0},{1,49},{17,33},{33,17},{49,1},{2,50}... | collective-permute-start | bytes 786440 | tf_op jit(solution)/shard_map/ppermute | solution.py:162
  235.1 24.0 %all-to-all-start.4 = ((bf16[32,16,640]{2,1,0:T(8,128)(2,1)}), bf16[32,16,640]{2,1,0:T(8,128)(2,1)S(1)}, u32[]{:S(2)}, u32[]{:S(2)}) async-start(bf16[32,16,640]{2,1,0:T(8,128)(2,1)} %bitcast.31), calls=%async_computation.4 | async-start | bytes 1310720 | tf_op jit(solution)/shard_map/all_to_all | solution.py:234
  248.8 45.3 %copy-start.14 = (s32[64,1]{0,1:T(1,128)S(1)}, s32[64,1]{0,1:T(1,128)}, u32[]{:S(2)}) copy-start(s32[64,1]{0,1:T(1,128)} %param.25) | copy-start | bytes 772
  279.2 15.7 %copy-start.9 = (f32[2,8]{1,0:T(2,128)}, f32[2,8]{1,0:T(2,128)S(1)}, u32[]{:S(2)}) copy-start(f32[2,8]{1,0:T(2,128)S(1)} %sub.57) | copy-start | bytes 196
  279.3 15.5 %copy-start.13 = (f32[2]{0:T(128)}, f32[2]{0:T(128)S(1)}, u32[]{:S(2)}) copy-start(f32[2]{0:T(128)S(1)} %broadcast_multiply_fusion) | copy-start | bytes 28
  279.9 12.9 %all-to-all-start.6 = ((f32[32,1,2]{2,1,0:T(1,128)}), f32[32,1,2]{2,1,0:T(1,128)S(1)}, u32[]{:S(2)}, u32[]{:S(2)}) async-start(f32[32,1,2]{2,1,0:T(1,128)} %broadcast_in_dim.94), calls=%async_computation.6 | async-start | bytes 32768 | tf_op jit(solution)/shard_map/all_to_all | solution.py:94
  (6 other events, 34.4 us)
Sparse Core Ops, SparseCore 0:
  10.5 131.2 all-gather.3

commit v5 on v3

--- a/solution.py
+++ b/solution.py
@@ -89,7 +89,7 @@
     blocks, _, width = weight_ref.shape
     rows = rows_ref[...]
     for j in range(blocks):
-        out_ref[j // 2, :, (j % 2) * width : (j % 2 + 1) * width] = jnp.dot(
+        out_ref[0, :, j * width : (j + 1) * width] = jnp.dot(
             rows, weight_ref[j], preferred_element_type=jnp.float32
         )
 
@@ -133,7 +133,7 @@
         cache.reshape(-1, head_width), "cont", axis=0, tiled=True
     )
     cached_keys, cached_values = gather_cache(prefix_keys), gather_cache(prefix_values)
-    window = lax.all_gather(after(out_weight, (weights, cached_keys, cached_values)), "cont")
+    window = lax.all_gather(after(out_weight, (cached_keys, cached_values)), "cont")
 
     inputs = states.astype(jnp.float32)
     squares = jnp.sum(everyone(jnp.sum(inputs * inputs, axis=-1), "prefix"), axis=0)
@@ -181,14 +181,19 @@
     cont_rows = path_count * SCORED
     scored_rows = everyone(context[path_length - SCORED :], "prefix").reshape(cont_rows, -1)
     sub_width = 2 * out_weight.shape[1]
+    depth, width = out_weight.shape
     pieces = pl.pallas_call(
         output_kernel,
+        grid=(tensors,),
+        in_specs=[
+            pl.BlockSpec(scored_rows.shape, lambda i: (0, 0)),
+            pl.BlockSpec((2, depth, width), lambda i: (i, 0, 0)),
+        ],
+        out_specs=pl.BlockSpec((1, cont_rows, sub_width), lambda i: (i, 0, 0)),
         out_shape=jax.ShapeDtypeStruct((tensors, cont_rows, sub_width), jnp.float32),
-        compiler_params=pltpu.CompilerParams(vmem_limit_bytes=24 * 1024 * 1024),
+        compiler_params=pltpu.CompilerParams(vmem_limit_bytes=56 * 1024 * 1024),
         cost_estimate=pl.CostEstimate(
-            flops=2 * scored_rows.size * window.shape[0] * window.shape[2],
-            bytes_accessed=2 * window.size,
-            transcendentals=0,
+            flops=2 * cont_rows * window.size, bytes_accessed=2 * window.size, transcendentals=0
         ),
     )(scored_rows, window)
     summed = jnp.sum(lax.all_to_all(pieces, "tensor", 0, 0), axis=0)
@@ -225,10 +230,11 @@
     mass_all = jnp.sum(shares[:, 1] * jnp.exp(shares[:, 0] - summit), axis=0)
     token_logprob = (jnp.sum(shares[:, 2], axis=0) - (summit + jnp.log(mass_all))).reshape(targets.shape)
     path_score = jnp.mean(token_logprob, axis=-1)
-    all_scores = everyone(path_score, ("tensor", "prefix")).reshape(-1)
     labels = jnp.arange(QUESTIONS, dtype=jnp.int32)
-    member = (questions[:, 0][:, None] == labels[None, :]).astype(jnp.float32)
-    question_score = jnp.sum(member * all_scores[:, None], axis=0) / jnp.sum(member, axis=0)
+    member = (questions[:, 0][None, :] == labels[:, None]).astype(jnp.float32)
+    share = (member / jnp.sum(member, axis=1, keepdims=True)).reshape(QUESTIONS, blocks, -1)
+    all_scores = everyone(path_score, ("tensor", "prefix"))
+    question_score = jnp.sum(share * all_scores.reshape(blocks, -1), axis=(1, 2))
     return (
         context[None, None],
         hidden.reshape(path_count, SCORED, 1, sub_width),

time: 286 us -> 289 us (1.010)
  blocking collectives: 114 us -> 86.4 us
  waiting for transfers between devices: 60 us -> 72.7 us
  starting transfers between devices: 63.6 us -> 73.7 us
  Pallas kernels: 7.05 us -> 12.1 us
    all_to_all x2 -> x0, blocking collectives: 25.9 us -> none  [everyone(): lax.all_to_all(jnp.broadcast_to(array[None], (size,) + array.shape), axis...]
    all_gather x1, waiting for transfers between devices: 1.08 us -> 25.2 us  [body(): lax.all_gather(after(out_weight, (cached_keys, cached_values)), 'cont')]
    all_gather x1, waiting for transfers between devices: 23.6 us -> 0.02 us  [body(): weights = lax.all_gather(lead, 'cont', axis=0, tiled=True)]
    all_to_all x2 -> x4, starting transfers between devices: 9.24 us -> 19.7 us  [everyone(): lax.all_to_all(jnp.broadcast_to(array[None], (size,) + array.shape), axis...]
    all_to_all x2 -> x4, waiting for transfers between devices: 6.31 us -> 16.3 us  [everyone(): lax.all_to_all(jnp.broadcast_to(array[None], (size,) + array.shape), axis...]
    pallas_call x1, Pallas kernels: 1.38 us -> 6.39 us  [body(): pl.pallas_call(output_kernel, grid=(tensors,), in_specs=[pl.BlockSpec(sco...]
  transfers between devices with their start and end apart: 14 -> 16, of which waited for: 7 -> 7; matrix products, arithmetic and copies ran while one was open for 4% -> 6% of each run, Pallas kernels for 2% -> 2%
where the time goes in v5:
time: 289 us; the launch traced here: 288 us
  blocking collectives  86.4 us (30%)
  starting transfers between devices  73.7 us (26%)
  waiting for transfers between devices  72.7 us (25%)
  between operations  17.8 us (6%)
  other arithmetic  12.2 us (4%)
  Pallas kernels  12.1 us (4%)
  local copies, waits for them, and re-layouts  6.71 us (2%)
  matrix products  5.96 us (2%)
    all_gather x2, blocking collectives, body(): lax.all_gather(cache.reshape(-1, head_width), 'cont', axis=0, tiled=True)  63.3 us
    all_gather x1, waiting for transfers between devices, body(): lax.all_gather(after(out_weight, (cached_keys, cached_values)), 'cont')  25.2 us
    all_gather x1, blocking collectives, body(): lax.all_gather(hidden, 'cont', axis=0, tiled=True).astype(jnp.float32)  23.1 us
    all_to_all x4, starting transfers between devices, everyone(): lax.all_to_all(jnp.broadcast_to(array[None], (size,) + array.shape), axis...  19.7 us
    all_to_all x4, waiting for transfers between devices, everyone(): lax.all_to_all(jnp.broadcast_to(array[None], (size,) + array.shape), axis...  16.3 us
    all_to_all x1, starting transfers between devices, body(): lax.all_to_all(payload.reshape(blocks, block_rows, vocab_block + lanes),...  13 us
    all_to_all x1, starting transfers between devices, body(): summed = jnp.sum(lax.all_to_all(pieces, 'tensor', 0, 0), axis=0)  13 us
    all_to_all x1, waiting for transfers between devices, body(): lax.all_to_all(payload.reshape(blocks, block_rows, vocab_block + lanes),...  12.4 us
  transfers between devices with their start and end apart: 16, of which 7 were waited for; matrix products, arithmetic and copies ran while one was open for 6% of the time, Pallas kernels for 2%

profile of v5, /device:TPU:1, one launch (start us, length us, event | category | flops | bytes accessed | tf_op | source)
XLA Modules:
  0.0 287.6 jit_solution(17919189991254455941)
XLA Ops:
  9.2 33.2 %all-gather = bf16[1,2048,1,128]{3,1,2,0:T(8,128)(2,1)S(1)} all-gather(bf16[1,128,1,128]{3,1,2,0:T(8,128)(2,1)} %param.18), channel_id=2, replica_groups=mesh['tensor'=8,'prefix'=4,'cont'=16] {'cont'}, dimensions={1}, use_global_device_ids=true | all-gather | bytes 557056 | tf_op jit(solution)/shard_map/all_gather | solution.py:132
  42.4 30.1 %all-gather.1 = bf16[1,2048,1,128]{3,1,2,0:T(8,128)(2,1)S(1)} all-gather(bf16[1,128,1,128]{3,1,2,0:T(8,128)(2,1)} %param.19), channel_id=3, replica_groups=mesh['tensor'=8,'prefix'=4,'cont'=16] {'cont'}, dimensions={1}, use_global_device_ids=true | all-gather | bytes 557056 | tf_op jit(solution)/shard_map/all_gather | solution.py:132
  72.6 4.4 %collective-permute-start.4 = (bf16[2048,128]{1,0:T(8,128)(2,1)S(1)}, bf16[2048,128]{1,0:T(8,128)(2,1)}, u32[]{:S(2)}, u32[]{:S(2)}) collective-permute-start(bf16[2048,128]{1,0:T(8,128)(2,1)S(1)} %bitcast.59), channel_id=1, source_target_pairs={{0,16},{16,0},{32,48},{48,32},{1,17},{17,1},{33,49},{49,33},{2,18}... | collective-permute-start | bytes 1572872 | tf_op jit(solution)/shard_map/ppermute | solution.py:158
  77.0 3.8 %collective-permute-start.6 = (bf16[2048,128]{1,0:T(8,128)(2,1)S(1)}, bf16[2048,128]{1,0:T(8,128)(2,1)}, u32[]{:S(2)}, u32[]{:S(2)}) collective-permute-start(bf16[2048,128]{1,0:T(8,128)(2,1)S(1)} %bitcast.58), channel_id=1, source_target_pairs={{0,48},{16,32},{32,16},{48,0},{1,49},{17,33},{33,17},{49,1},{2,50}... | collective-permute-start | bytes 1572872 | tf_op jit(solution)/shard_map/ppermute | solution.py:158
  81.8 3.2 %all-to-all-start = ((f32[4,4,128]{2,1,0:T(4,128)}), f32[4,4,128]{2,1,0:T(4,128)S(1)}, u32[]{:S(2)}, u32[]{:S(2)}) async-start(f32[4,4,128]{2,1,0:T(4,128)} %broadcast_in_dim.54), calls=%async_computation | async-start | bytes 16384 | tf_op jit(solution)/shard_map/all_to_all | solution.py:103
  90.8 4.5 %collective-permute-start.5 = (bf16[2048,128]{1,0:T(8,128)(2,1)}, bf16[2048,128]{1,0:T(8,128)(2,1)}, u32[]{:S(2)}, u32[]{:S(2)}) collective-permute-start(bf16[2048,128]{1,0:T(8,128)(2,1)} %broadcast_select_fusion.1), channel_id=1, source_target_pairs={{0,48},{16,32},{32,16},{48,0},{1,49},{17,33},{33,17},{49,1},{2,50}... | collective-permute-start | bytes 1572872 | tf_op jit(solution)/shard_map/ppermute | solution.py:160
  99.3 3.7 %fusion.3 = f32[4,128,640]{2,1,0:T(8,128)S(1)} fusion(bf16[2048,1280]{1,0:T(8,128)(2,1)} %all-gather.6.cloned.1.call-done, bf16[4,128,2048]{2,1,0:T(8,128)(2,1)S(1)} %copy-done.1, f32[2048]{0:T(1024)S(1)} %copy-done.10, f32[4,128]{1,0:T(4,128)S(1)} %add_rsqrt_fusion), kind=kOutput, calls=%fused_computation.6 | convolution fusion | flops 1346371584 | bytes 6039552 | tf_op jit(solution)/shard_map/dot_general | solution.py:145
  111.6 8.6 %collective-permute-done.2 = f32[2,128,640]{2,1,0:T(8,128)S(1)} collective-permute-done((f32[2,128,640]{2,1,0:T(8,128)S(1)}, f32[2,128,640]{2,1,0:T(8,128)S(1)}, u32[]{:S(2)}, u32[]{:S(2)}) %collective-permute-start.2) | collective-permute-done | bytes 655392 | tf_op jit(solution)/shard_map/ppermute | solution.py:170
  120.2 3.6 %collective-permute-start.3 = (f32[128,640]{1,0:T(8,128)S(1)}, f32[128,640]{1,0:T(8,128)S(1)}, u32[]{:S(2)}, u32[]{:S(2)}) collective-permute-start(f32[128,640]{1,0:T(8,128)S(1)} %fusion.9), channel_id=1, source_target_pairs={{0,16},{16,0},{32,48},{48,32},{1,17},{17,1},{33,49},{49,33},{2,18}... | collective-permute-start | bytes 983048 | tf_op jit(solution)/shard_map/ppermute | solution.py:171
  123.9 4.5 %collective-permute-start.1 = (f32[128,640]{1,0:T(8,128)S(1)}, f32[128,640]{1,0:T(8,128)S(1)}, u32[]{:S(2)}, u32[]{:S(2)}) collective-permute-start(f32[128,640]{1,0:T(8,128)S(1)} %fusion.12), channel_id=1, source_target_pairs={{0,48},{16,32},{32,16},{48,0},{1,49},{17,33},{33,17},{49,1},{2,50}... | collective-permute-start | bytes 983048 | tf_op jit(solution)/shard_map/ppermute | solution.py:171
  129.5 3.6 %collective-permute-done.1 = f32[128,640]{1,0:T(8,128)S(1)} collective-permute-done((f32[128,640]{1,0:T(8,128)S(1)}, f32[128,640]{1,0:T(8,128)S(1)}, u32[]{:S(2)}, u32[]{:S(2)}) %collective-permute-start.1) | collective-permute-done | bytes 327712 | tf_op jit(solution)/shard_map/ppermute | solution.py:171
  133.6 5.7 %shard_map.164 = bf16[128,1024]{1,0:T(8,128)(2,1)} custom-call(f32[128,1024]{1,0:T(8,128)S(1)} %pad_maximum_fusion.3.q_ref, f32[128,128]{1,0:T(8,128)S(1)} %get-tuple-element.23.cos_ref, f32[128,128]{1,0:T(8,128)S(1)} %get-tuple-element.16.sin_ref, bf16[128,128]{1,0:T(8,128)(2,1)S(1)} %get-tuple-element.15.kf_ref, bf16[128,128]{1,0:T(8,128)(2,1)S(1)} %slice.141.vf_ref, ...), custom_call_target="tpu_custom_call" | custom-call | flops 1140850688 | bytes 2097152 | tf_op jit(solution)/shard_map/pallas_call | solution.py:67
  140.6 4.0 %all-to-all-start.1 = ((bf16[4,8,1024]{2,1,0:T(8,128)(2,1)}), bf16[4,8,1024]{2,1,0:T(8,128)(2,1)S(1)}, u32[]{:S(2)}, u32[]{:S(2)}) async-start(bf16[4,8,1024]{2,1,0:T(8,128)(2,1)} %broadcast_in_dim.56), calls=%async_computation.1 | async-start | bytes 131072 | tf_op jit(solution)/shard_map/all_to_all | solution.py:103
  144.6 25.2 %all-gather.8.cloned.1.call-done = bf16[16384,128]{1,0:T(8,128)(2,1)} async-done(((bf16[1024,128]{1,0:T(8,128)(2,1)}), bf16[16384,128]{1,0:T(8,128)(2,1)}) %all-gather.8.cloned.1.call-update) | async-done | bytes 4194320 | tf_op jit(solution)/shard_map/all_gather | solution.py:136
  170.4 6.4 %shard_map.165 = f32[8,32,256]{2,1,0:T(8,128)} custom-call(bf16[32,1024]{1,0:T(8,128)(2,1)} %bitcast.61, bf16[16,1024,128]{2,1,0:T(8,128)(2,1)} %bitcast.60), custom_call_target="tpu_custom_call" | custom-call | flops 134217728 | bytes 4194304 | tf_op jit(solution)/shard_map/pallas_call | solution.py:185
  176.8 13.0 %all-to-all-start.2 = ((f32[8,32,256]{2,1,0:T(8,128)}), f32[8,32,256]{2,1,0:T(8,128)S(1)}, u32[]{:S(2)}, u32[]{:S(2)}) async-start(f32[8,32,256]{2,1,0:T(8,128)} %shard_map.165), calls=%async_computation.2 | async-start | bytes 524288 | tf_op jit(solution)/shard_map/all_to_all | solution.py:199
  189.8 6.5 %all-to-all-done.2 = f32[8,32,256]{2,1,0:T(8,128)S(1)} async-done(((f32[8,32,256]{2,1,0:T(8,128)}), f32[8,32,256]{2,1,0:T(8,128)S(1)}, u32[]{:S(2)}, u32[]{:S(2)}) %all-to-all-start.2) | async-done | bytes 262176 | tf_op jit(solution)/shard_map/all_to_all | solution.py:199
  196.3 23.1 %all_gather.23 = bf16[512,256]{1,0:T(8,128)(2,1)S(1)} all-gather(bf16[32,256]{1,0:T(8,128)(2,1)S(1)} %fusion.22), channel_id=1, replica_groups=mesh['tensor'=8,'prefix'=4,'cont'=16] {'cont'}, dimensions={0}, use_global_device_ids=true | all-gather | bytes 278528 | tf_op jit(solution)/shard_map/all_gather | solution.py:203
  221.3 13.0 %all-to-all-start.3 = ((bf16[32,16,640]{2,1,0:T(8,128)(2,1)}), bf16[32,16,640]{2,1,0:T(8,128)(2,1)S(1)}, u32[]{:S(2)}, u32[]{:S(2)}) async-start(bf16[32,16,640]{2,1,0:T(8,128)(2,1)} %bitcast.19), calls=%async_computation.3 | async-start | bytes 1310720 | tf_op jit(solution)/shard_map/all_to_all | solution.py:216
  234.4 12.4 %all-to-all-done.3 = bf16[32,16,640]{2,1,0:T(8,128)(2,1)S(1)} async-done(((bf16[32,16,640]{2,1,0:T(8,128)(2,1)}), bf16[32,16,640]{2,1,0:T(8,128)(2,1)S(1)}, u32[]{:S(2)}, u32[]{:S(2)}) %all-to-all-start.3) | async-done | bytes 655392 | tf_op jit(solution)/shard_map/all_to_all | solution.py:216
  248.2 6.4 %all-to-all-start.4 = ((f32[16,3,16]{2,1,0:T(4,128)}), f32[16,3,16]{2,1,0:T(4,128)S(1)}, u32[]{:S(2)}, u32[]{:S(2)}) async-start(f32[16,3,16]{2,1,0:T(4,128)} %broadcast_in_dim.63), calls=%async_computation.4 | async-start | bytes 65536 | tf_op jit(solution)/shard_map/all_to_all | solution.py:103
  256.1 10.0 %all-to-all-done.4 = f32[16,3,16]{2,1,0:T(4,128)S(1)} async-done(((f32[16,3,16]{2,1,0:T(4,128)}), f32[16,3,16]{2,1,0:T(4,128)S(1)}, u32[]{:S(2)}, u32[]{:S(2)}) %all-to-all-start.4) | async-done | bytes 3104 | tf_op jit(solution)/shard_map/all_to_all | solution.py:103
  267.0 6.0 %all-to-all-start.5 = ((f32[32,1,2]{2,1,0:T(1,128)}), f32[32,1,2]{2,1,0:T(1,128)S(1)}, u32[]{:S(2)}, u32[]{:S(2)}) async-start(f32[32,1,2]{2,1,0:T(1,128)} %broadcast_in_dim.96), calls=%async_computation.5 | async-start | bytes 32768 | tf_op jit(solution)/shard_map/all_to_all | solution.py:103
  273.6 6.3 %all-to-all-done.5 = f32[32,1,2]{2,1,0:T(1,128)S(1)} async-done(((f32[32,1,2]{2,1,0:T(1,128)}), f32[32,1,2]{2,1,0:T(1,128)S(1)}, u32[]{:S(2)}, u32[]{:S(2)}) %all-to-all-start.5) | async-done | bytes 288 | tf_op jit(solution)/shard_map/all_to_all | solution.py:103
  (104 shorter events, 28.5 us)
Async XLA Ops:
  7.2 212.4 %copy-start = (bf16[1,256,512]{2,1,0:T(8,128)(2,1)S(1)}, bf16[1,256,512]{2,1,0:T(8,128)(2,1)}, u32[]{:S(2)}) copy-start(bf16[1,256,512]{2,1,0:T(8,128)(2,1)} %param.23) | copy-start | bytes 786436
  7.2 73.5 %copy-start.1 = (bf16[4,128,2048]{2,1,0:T(8,128)(2,1)S(1)}, bf16[4,128,2048]{2,1,0:T(8,128)(2,1)}, u32[]{:S(2)}) copy-start(bf16[4,128,2048]{2,1,0:T(8,128)(2,1)} %param.13) | copy-start | bytes 6291460
  7.2 92.0 %all-gather.6.cloned.1.call-start = ((), (), s32[]{:S(2)}) async-start(), calls=%async_computation.6 | async-start | bytes 5570560 | tf_op jit(solution)/shard_map/all_gather | solution.py:131
  9.1 76.9 %copy-start.4 = (s32[4]{0:T(128)S(1)}, s32[4]{0:T(128)}, u32[]{:S(2)}) copy-start(s32[4]{0:T(128)} %param.20) | copy-start | bytes 52
  9.2 160.6 %all-gather.8.cloned.1.call-start = ((), (), s32[]{:S(2)}) async-start(), calls=%async_computation.7 | async-start | bytes 4456448 | tf_op jit(solution)/shard_map/all_gather | solution.py:136
  72.6 17.4 %collective-permute-start.4 = (bf16[2048,128]{1,0:T(8,128)(2,1)S(1)}, bf16[2048,128]{1,0:T(8,128)(2,1)}, u32[]{:S(2)}, u32[]{:S(2)}) collective-permute-start(bf16[2048,128]{1,0:T(8,128)(2,1)S(1)} %bitcast.59), channel_id=1, source_target_pairs={{0,16},{16,0},{32,48},{48,32},{1,17},{17,1},{33,49},{49,33},{2,18}... | collective-permute-start | bytes 1572872 | tf_op jit(solution)/shard_map/ppermute | solution.py:158
  77.0 18.4 %collective-permute-start.6 = (bf16[2048,128]{1,0:T(8,128)(2,1)S(1)}, bf16[2048,128]{1,0:T(8,128)(2,1)}, u32[]{:S(2)}, u32[]{:S(2)}) collective-permute-start(bf16[2048,128]{1,0:T(8,128)(2,1)S(1)} %bitcast.58), channel_id=1, source_target_pairs={{0,48},{16,32},{32,16},{48,0},{1,49},{17,33},{33,17},{49,1},{2,50}... | collective-permute-start | bytes 1572872 | tf_op jit(solution)/shard_map/ppermute | solution.py:158
  81.8 8.1 %all-to-all-start = ((f32[4,4,128]{2,1,0:T(4,128)}), f32[4,4,128]{2,1,0:T(4,128)S(1)}, u32[]{:S(2)}, u32[]{:S(2)}) async-start(f32[4,4,128]{2,1,0:T(4,128)} %broadcast_in_dim.54), calls=%async_computation | async-start | bytes 16384 | tf_op jit(solution)/shard_map/all_to_all | solution.py:103
  90.8 19.6 %collective-permute-start.5 = (bf16[2048,128]{1,0:T(8,128)(2,1)}, bf16[2048,128]{1,0:T(8,128)(2,1)}, u32[]{:S(2)}, u32[]{:S(2)}) collective-permute-start(bf16[2048,128]{1,0:T(8,128)(2,1)} %broadcast_select_fusion.1), channel_id=1, source_target_pairs={{0,48},{16,32},{32,16},{48,0},{1,49},{17,33},{33,17},{49,1},{2,50}... | collective-permute-start | bytes 1572872 | tf_op jit(solution)/shard_map/ppermute | solution.py:160
  97.3 13.1 %collective-permute-start.7 = (bf16[2048,128]{1,0:T(8,128)(2,1)}, bf16[2048,128]{1,0:T(8,128)(2,1)}, u32[]{:S(2)}, u32[]{:S(2)}) collective-permute-start(bf16[2048,128]{1,0:T(8,128)(2,1)} %broadcast_select_fusion), channel_id=1, source_target_pairs={{0,16},{16,0},{32,48},{48,32},{1,17},{17,1},{33,49},{49,33},{2,18}... | collective-permute-start | bytes 1572872 | tf_op jit(solution)/shard_map/ppermute | solution.py:160
  103.1 17.1 %collective-permute-start.2 = (f32[2,128,640]{2,1,0:T(8,128)S(1)}, f32[2,128,640]{2,1,0:T(8,128)S(1)}, u32[]{:S(2)}, u32[]{:S(2)}) collective-permute-start(f32[2,128,640]{2,1,0:T(8,128)S(1)} %pad_maximum_fusion.1), channel_id=1, source_target_pairs={{0,48},{16,32},{32,16},{48,0},{1,49},{17,33},{33,17},{49,1},{2,50}... | collective-permute-start | bytes 1966088 | tf_op jit(solution)/shard_map/ppermute | solution.py:170
  107.6 16.2 %collective-permute-start = (f32[2,128,640]{2,1,0:T(8,128)S(1)}, f32[2,128,640]{2,1,0:T(8,128)S(1)}, u32[]{:S(2)}, u32[]{:S(2)}) collective-permute-start(f32[2,128,640]{2,1,0:T(8,128)S(1)} %pad_maximum_fusion), channel_id=1, source_target_pairs={{0,16},{16,0},{32,48},{48,32},{1,17},{17,1},{33,49},{49,33},{2,18}... | collective-permute-start | bytes 1966088 | tf_op jit(solution)/shard_map/ppermute | solution.py:170
  120.2 13.0 %collective-permute-start.3 = (f32[128,640]{1,0:T(8,128)S(1)}, f32[128,640]{1,0:T(8,128)S(1)}, u32[]{:S(2)}, u32[]{:S(2)}) collective-permute-start(f32[128,640]{1,0:T(8,128)S(1)} %fusion.9), channel_id=1, source_target_pairs={{0,16},{16,0},{32,48},{48,32},{1,17},{17,1},{33,49},{49,33},{2,18}... | collective-permute-start | bytes 983048 | tf_op jit(solution)/shard_map/ppermute | solution.py:171
  123.9 9.2 %collective-permute-start.1 = (f32[128,640]{1,0:T(8,128)S(1)}, f32[128,640]{1,0:T(8,128)S(1)}, u32[]{:S(2)}, u32[]{:S(2)}) collective-permute-start(f32[128,640]{1,0:T(8,128)S(1)} %fusion.12), channel_id=1, source_target_pairs={{0,48},{16,32},{32,16},{48,0},{1,49},{17,33},{33,17},{49,1},{2,50}... | collective-permute-start | bytes 983048 | tf_op jit(solution)/shard_map/ppermute | solution.py:171
  140.6 29.2 %all-to-all-start.1 = ((bf16[4,8,1024]{2,1,0:T(8,128)(2,1)}), bf16[4,8,1024]{2,1,0:T(8,128)(2,1)S(1)}, u32[]{:S(2)}, u32[]{:S(2)}) async-start(bf16[4,8,1024]{2,1,0:T(8,128)(2,1)} %broadcast_in_dim.56), calls=%async_computation.1 | async-start | bytes 131072 | tf_op jit(solution)/shard_map/all_to_all | solution.py:103
  170.4 49.2 %copy-start.5 = (f32[1,256]{1,0:T(1,128)S(1)}, f32[1,256]{1,0:T(1,128)}, u32[]{:S(2)}) copy-start(f32[1,256]{1,0:T(1,128)} %param.22) | copy-start | bytes 3076
  176.8 19.5 %all-to-all-start.2 = ((f32[8,32,256]{2,1,0:T(8,128)}), f32[8,32,256]{2,1,0:T(8,128)S(1)}, u32[]{:S(2)}, u32[]{:S(2)}) async-start(f32[8,32,256]{2,1,0:T(8,128)} %shard_map.165), calls=%async_computation.2 | async-start | bytes 524288 | tf_op jit(solution)/shard_map/all_to_all | solution.py:199
  220.0 14.3 %copy-start.6 = (s32[2,8]{1,0:T(2,128)S(1)}, s32[2,8]{1,0:T(2,128)}, u32[]{:S(2)}) copy-start(s32[2,8]{1,0:T(2,128)} %param.24) | copy-start | bytes 196
  220.1 34.5 %copy-start.11 = (s32[64,1]{0,1:T(1,128)S(1)}, s32[64,1]{0,1:T(1,128)}, u32[]{:S(2)}) copy-start(s32[64,1]{0,1:T(1,128)} %param.25) | copy-start | bytes 772
  221.3 25.6 %all-to-all-start.3 = ((bf16[32,16,640]{2,1,0:T(8,128)(2,1)}), bf16[32,16,640]{2,1,0:T(8,128)(2,1)S(1)}, u32[]{:S(2)}, u32[]{:S(2)}) async-start(bf16[32,16,640]{2,1,0:T(8,128)(2,1)} %bitcast.19), calls=%async_computation.3 | async-start | bytes 1310720 | tf_op jit(solution)/shard_map/all_to_all | solution.py:216
  248.2 17.9 %all-to-all-start.4 = ((f32[16,3,16]{2,1,0:T(4,128)}), f32[16,3,16]{2,1,0:T(4,128)S(1)}, u32[]{:S(2)}, u32[]{:S(2)}) async-start(f32[16,3,16]{2,1,0:T(4,128)} %broadcast_in_dim.63), calls=%async_computation.4 | async-start | bytes 65536 | tf_op jit(solution)/shard_map/all_to_all | solution.py:103
  266.3 14.5 %copy-start.7 = (f32[2,8]{1,0:T(2,128)}, f32[2,8]{1,0:T(2,128)S(1)}, u32[]{:S(2)}) copy-start(f32[2,8]{1,0:T(2,128)S(1)} %sub.57) | copy-start | bytes 196
  266.4 14.3 %copy-start.8 = (f32[2]{0:T(128)}, f32[2]{0:T(128)S(1)}, u32[]{:S(2)}) copy-start(f32[2]{0:T(128)S(1)} %broadcast_multiply_fusion) | copy-start | bytes 28
  267.0 12.9 %all-to-all-start.5 = ((f32[32,1,2]{2,1,0:T(1,128)}), f32[32,1,2]{2,1,0:T(1,128)S(1)}, u32[]{:S(2)}, u32[]{:S(2)}) async-start(f32[32,1,2]{2,1,0:T(1,128)} %broadcast_in_dim.96), calls=%async_computation.5 | async-start | bytes 32768 | tf_op jit(solution)/shard_map/all_to_all | solution.py:103
  (4 other events, 20.2 us)
Sparse Core Ops, SparseCore 0:
  10.1 87.7 all-gather.5
  100.0 69.7 all-gather.7
